TPU v7x, 32 devices: a whole 2x2x4 slice. The times are simulated.
32 devices in a mesh: wide: 16 (over z, y, core), narrow: 2 (over x).
Axes of the slice: x: 2, y: 2, z: 4, core: 2. Of those that a mesh axis runs over, the one named last changes fastest.
Arguments:
- target: bfloat16 [16, 512, 512], P('wide', 'narrow'), may hold values from -6 to 6
- memory: bfloat16 [16, 512, 512], P('wide', 'narrow'), may hold values from -6 to 6
- target_lens: int32 [16, 8], P('wide'), may hold values from 1 to 384, as said below
- source_lens: int32 [16, 8], P('wide'), may hold values from 1 to 384, as said below
- self_in: bfloat16 [512, 1536], replicated, may hold values from -0.25 to 0.25
- self_out: bfloat16 [512, 512], replicated, may hold values from -1 to 1
- cross_q: bfloat16 [512, 512], replicated, may hold values from -0.25 to 0.25
- cross_kv: bfloat16 [512, 1024], replicated, may hold values from -0.25 to 0.25
- cross_out: bfloat16 [512, 512], replicated, may hold values from -1 to 1
- ffn_in: bfloat16 [512, 2048], replicated, may hold values from -0.25 to 0.25
- ffn_in_bias: float32 [2048], replicated, may hold values from -3 to 3
- ffn_out: bfloat16 [2048, 512], replicated, may hold values from -0.125 to 0.125
- ffn_out_bias: float32 [512], replicated, may hold values from -3 to 3
- norm_gain: float32 [3, 512], replicated, may hold values from 0.1 to 1.9
- norm_bias: float32 [3, 512], replicated, may hold values from -3 to 3
- cotangent: bfloat16 [16, 512, 512], P('wide', 'narrow'), may hold values from -6 to 6
Outputs:
- output: bfloat16 [16, 512, 512], P('wide', 'narrow')
- target_grad: float32 [16, 512, 512], P('wide', 'narrow')
- memory_grad: float32 [16, 512, 512], P('wide', 'narrow')
- self_in_grad: float32 [512, 1536], P('narrow')
- self_out_grad: float32 [512, 512], P('narrow')
- cross_q_grad: float32 [512, 512], P('narrow')
- cross_kv_grad: float32 [512, 1024], P('narrow')
- cross_out_grad: float32 [512, 512], P('narrow')
- ffn_in_grad: float32 [512, 2048], P('narrow')
- ffn_in_bias_grad: float32 [2048], P('narrow')
- ffn_out_grad: float32 [2048, 512], P('narrow')
- ffn_out_bias_grad: float32 [512], P('narrow')
- norm_gain_grad: float32 [3, 512], P(None, 'narrow')
- norm_bias_grad: float32 [3, 512], P(None, 'narrow')
Inputs may be any that keep to these rules, and one draw needn't show every extreme that they name: `target_lens`: row b holds 8 target documents in order with these lengths; positions after their sum are padding. Target document j attends to source document j. `source_lens`: row b holds 8 source documents in order with these lengths; positions after their sum are padding.
All inputs are finite; a program needn't handle non-finite values.
Results may differ from a plain program's by a relative error of at most 0.025.
Values may be sent and summed in bfloat16 or wider, within the bound.
No kernel may reach another device: no remote copies, remote signals or barrier semaphores. Data moves between devices by JAX's collectives and lax.ppermute only.
A program may use at most 128 MiB of HBM per device.

v0:
```python
import math

import jax
import jax.numpy as jnp
from jax import lax
from jax.sharding import PartitionSpec as P

HEADS = 8
HEAD_DIM = 64


EPSILON = 1e-05
MASKED = -1e30


def segment_ids(doc_lens, length):
    ends = jnp.cumsum(doc_lens, axis=-1)
    places = jnp.arange(length, dtype=jnp.int32)
    return jnp.sum((places[:, None] >= ends[..., None, :]).astype(jnp.int32), axis=-1)


def layer_norm(values, gain, shift):
    centre = values - jnp.mean(values, axis=-1, keepdims=True)
    spread = jnp.mean(centre * centre, axis=-1, keepdims=True)
    return centre * lax.rsqrt(spread + EPSILON) * gain + shift


def gelu_tanh(values):
    return jax.nn.gelu(values, approximate=True)


def project(activity, weight):
    return jnp.einsum("rsd,de->rse", activity, weight, preferred_element_type=jnp.float32)


def project_back(gradient, weight):
    return jnp.einsum("rse,de->rsd", gradient, weight, preferred_element_type=jnp.float32)


def weight_grad(activity, gradient):
    return jnp.einsum("rsd,rse->de", activity, gradient, preferred_element_type=jnp.float32)


def split_heads(values):
    return values.reshape(values.shape[0], values.shape[1], HEADS, HEAD_DIM)


def join_heads(values):
    return values.reshape(values.shape[0], values.shape[1], HEADS * HEAD_DIM)


def block_scores(query_heads, key_heads, query_seg, key_seg, query_pos, key_pos, causal):
    raw_scores = jnp.einsum(
        "rqhd,rkhd->rhqk", query_heads, key_heads, preferred_element_type=jnp.float32
    )
    visible = query_seg[:, :, None] == key_seg[:, None, :]
    if causal:
        visible = visible & (key_pos[None, None, :] <= query_pos[None, :, None])
    return jnp.where(visible[:, None], raw_scores * HEAD_DIM ** (-0.5), MASKED)


def block_backward(query_heads, grad_heads, key_heads, value_heads, scores, log_norm, row_dot):
    attention = jnp.exp(scores - log_norm[..., None])
    grad_attn = jnp.einsum(
        "rqhd,rkhd->rhqk", grad_heads, value_heads, preferred_element_type=jnp.float32
    )
    grad_scores = (attention * (grad_attn - row_dot[..., None]) * HEAD_DIM ** (-0.5)).astype(
        jnp.bfloat16
    )
    grad_query = jnp.einsum(
        "rhqk,rkhd->rqhd", grad_scores, key_heads, preferred_element_type=jnp.float32
    )
    grad_key = jnp.einsum(
        "rhqk,rqhd->rkhd", grad_scores, query_heads, preferred_element_type=jnp.float32
    )
    grad_value = jnp.einsum(
        "rhqk,rqhd->rkhd",
        attention.astype(jnp.bfloat16),
        grad_heads,
        preferred_element_type=jnp.float32,
    )
    return (grad_query, jnp.concatenate([join_heads(grad_key), join_heads(grad_value)], axis=-1))


def make_key_fold(query_heads, query_seg, key_seg_full, query_pos, causal, running, portion):
    run_max, run_sum, stored = running
    span_len = portion.shape[1]
    key_pos = jnp.arange(span_len, dtype=jnp.int32)
    scores = block_scores(
        query_heads,
        split_heads(portion[:, :, : HEADS * HEAD_DIM]),
        query_seg,
        key_seg_full,
        query_pos,
        key_pos,
        causal,
    )
    new_max = jnp.maximum(run_max, jnp.max(scores, axis=-1))
    run_sum = jnp.sum(jnp.exp(scores - new_max[..., None]), axis=-1)
    stored = portion
    return (new_max, run_sum, stored)


def attend_stored(query_heads, stored, query_seg, key_seg_full, query_pos, causal, log_norm):
    total_len = stored.shape[1]
    pair_half = stored.shape[2] // 2
    block_len = math.gcd(total_len, max(query_heads.shape[1], 512))

    def advance(low_sum, block_idx):
        begin_at = block_idx * block_len
        portion = lax.dynamic_slice_in_dim(stored, begin_at, block_len, 1)
        key_seg = lax.dynamic_slice_in_dim(key_seg_full, begin_at, block_len, 1)
        key_pos = begin_at + jnp.arange(block_len, dtype=jnp.int32)
        value_heads = split_heads(portion[:, :, pair_half:])
        scores = block_scores(
            query_heads,
            split_heads(portion[:, :, :pair_half]),
            query_seg,
            key_seg,
            query_pos,
            key_pos,
            causal,
        )
        attention = jnp.exp(scores - log_norm[..., None])
        low_sum = low_sum + jnp.einsum(
            "rhqk,rkhd->rqhd",
            attention.astype(jnp.bfloat16),
            value_heads,
            preferred_element_type=jnp.float32,
        )
        return (low_sum, None)

    zeros_q = jnp.zeros(query_heads.shape, jnp.float32)
    low_sum, _ = lax.scan(advance, zeros_q, jnp.arange(total_len // block_len, dtype=jnp.int32))
    return low_sum


def attend_back_stored(
    query_heads, grad_heads, stored, query_seg, key_seg_full, query_pos, causal, log_norm, row_dot
):
    total_len = stored.shape[1]
    pair_half = stored.shape[2] // 2
    block_len = math.gcd(total_len, max(query_heads.shape[1], 512))

    def advance(block_idx, running):
        grad_query, grad_term = running
        begin_at = block_idx * block_len
        portion = lax.dynamic_slice_in_dim(stored, begin_at, block_len, 1)
        key_seg = lax.dynamic_slice_in_dim(key_seg_full, begin_at, block_len, 1)
        key_pos = begin_at + jnp.arange(block_len, dtype=jnp.int32)
        key_heads = split_heads(portion[:, :, :pair_half])
        value_heads = split_heads(portion[:, :, pair_half:])
        scores = block_scores(
            query_heads, key_heads, query_seg, key_seg, query_pos, key_pos, causal
        )
        block_dq, block_dkv = block_backward(
            query_heads, grad_heads, key_heads, value_heads, scores, log_norm, row_dot
        )
        grad_term = lax.dynamic_update_slice_in_dim(grad_term, block_dkv, begin_at, 1)
        return (grad_query + block_dq, grad_term)

    start_vals = (jnp.zeros(query_heads.shape, jnp.float32), jnp.zeros(stored.shape, jnp.float32))
    grad_query, grad_term = lax.fori_loop(0, total_len // block_len, advance, start_vals)
    return (join_heads(grad_query), grad_term)


def local(
    target,
    memory,
    target_lens,
    source_lens,
    self_in,
    self_out,
    cross_q,
    cross_kv,
    cross_out,
    ffn_in,
    ffn_in_bias,
    ffn_out,
    ffn_out_bias,
    norm_gain,
    norm_bias,
    cotangent,
):
    row_count, shard_len, feat_width = target.shape
    total_len = shard_len * lax.axis_size("narrow")
    own_start = lax.axis_index("narrow") * shard_len
    own_pos = own_start + jnp.arange(shard_len, dtype=jnp.int32)
    target_seg = segment_ids(target_lens, total_len)
    source_seg = segment_ids(source_lens, total_len)
    target_own = lax.dynamic_slice_in_dim(target_seg, own_start, shard_len, 1)
    start_state = (
        jnp.full((row_count, HEADS, shard_len), MASKED, jnp.float32),
        jnp.zeros((row_count, HEADS, shard_len), jnp.float32),
        jnp.zeros((row_count, total_len, 2 * feat_width), jnp.bfloat16),
    )
    triple = project(target, self_in).astype(jnp.bfloat16)
    self_query = split_heads(triple[:, :, :feat_width])
    self_pairs = triple[:, :, feat_width:]
    self_max, self_sum, self_store = make_key_fold(
        self_query,
        target_own,
        target_seg,
        own_pos,
        True,
        start_state,
        lax.all_gather(self_pairs, "narrow", axis=1, tiled=True),
    )
    self_norm = self_max + jnp.log(self_sum)
    self_low = attend_stored(
        self_query, self_store, target_own, target_seg, own_pos, True, self_norm
    )
    self_mix = join_heads(self_low).astype(jnp.bfloat16)
    first, first_pull = jax.vjp(
        layer_norm,
        target.astype(jnp.float32) + project(self_mix, self_out),
        norm_gain[0],
        norm_bias[0],
    )
    first_low = first.astype(jnp.bfloat16)
    cross_query = split_heads(project(first_low, cross_q).astype(jnp.bfloat16))
    cross_pairs = project(memory, cross_kv).astype(jnp.bfloat16)
    cross_max, cross_sum, cross_store = make_key_fold(
        cross_query,
        target_own,
        source_seg,
        own_pos,
        False,
        start_state,
        lax.all_gather(cross_pairs, "narrow", axis=1, tiled=True),
    )
    cross_norm = cross_max + jnp.log(cross_sum)
    cross_low = attend_stored(
        cross_query, cross_store, target_own, source_seg, own_pos, False, cross_norm
    )
    cross_mix = join_heads(cross_low).astype(jnp.bfloat16)
    second, second_pull = jax.vjp(
        layer_norm, first + project(cross_mix, cross_out), norm_gain[1], norm_bias[1]
    )
    second_low = second.astype(jnp.bfloat16)
    inner = project(second_low, ffn_in) + ffn_in_bias
    active, gelu_pull = jax.vjp(gelu_tanh, inner)
    active_low = active.astype(jnp.bfloat16)
    result, third_pull = jax.vjp(
        layer_norm, second + project(active_low, ffn_out) + ffn_out_bias, norm_gain[2], norm_bias[2]
    )
    grad_third, gain_third, shift_third = third_pull(cotangent.astype(jnp.float32))
    grad_outer = grad_third.astype(jnp.bfloat16)
    ffn_out_g = weight_grad(active_low, grad_outer)
    ffn_out_bias_g = jnp.sum(grad_third, axis=(0, 1))
    (grad_active,) = gelu_pull(project_back(grad_outer, ffn_out))
    grad_inner = grad_active.astype(jnp.bfloat16)
    ffn_in_g = weight_grad(second_low, grad_inner)
    ffn_in_bias_g = jnp.sum(grad_active, axis=(0, 1))
    grad_second, gain_second, shift_second = second_pull(
        grad_third + project_back(grad_inner, ffn_in)
    )
    grad_cross = grad_second.astype(jnp.bfloat16)
    cross_out_g = weight_grad(cross_mix, grad_cross)
    cross_dout = split_heads(project_back(grad_cross, cross_out).astype(jnp.bfloat16))
    cross_dot = jnp.swapaxes(jnp.sum(cross_dout.astype(jnp.float32) * cross_low, axis=-1), 1, 2)
    cross_dq, cross_term = attend_back_stored(
        cross_query,
        cross_dout,
        cross_store,
        target_own,
        source_seg,
        own_pos,
        False,
        cross_norm,
        cross_dot,
    )
    cross_dpairs = lax.psum_scatter(
        cross_term.astype(jnp.bfloat16), "narrow", scatter_dimension=1, tiled=True
    )
    cross_dq_low = cross_dq.astype(jnp.bfloat16)
    cross_q_g = weight_grad(first_low, cross_dq_low)
    cross_kv_g = weight_grad(memory, cross_dpairs)
    memory_grad = project_back(cross_dpairs, cross_kv)
    grad_first, gain_first, shift_first = first_pull(
        grad_second + project_back(cross_dq_low, cross_q)
    )
    grad_self = grad_first.astype(jnp.bfloat16)
    self_out_g = weight_grad(self_mix, grad_self)
    self_dout = split_heads(project_back(grad_self, self_out).astype(jnp.bfloat16))
    self_dot = jnp.swapaxes(jnp.sum(self_dout.astype(jnp.float32) * self_low, axis=-1), 1, 2)
    self_dq, self_term = attend_back_stored(
        self_query,
        self_dout,
        self_store,
        target_own,
        target_seg,
        own_pos,
        True,
        self_norm,
        self_dot,
    )
    self_dpairs = lax.psum_scatter(
        self_term.astype(jnp.bfloat16), "narrow", scatter_dimension=1, tiled=True
    ).astype(jnp.float32)
    grad_triple = jnp.concatenate([self_dq, self_dpairs], axis=-1).astype(jnp.bfloat16)
    self_in_g = weight_grad(target, grad_triple)
    target_grad = grad_first + project_back(grad_triple, self_in)
    gain_g = jnp.stack([gain_first, gain_second, gain_third])
    shift_g = jnp.stack([shift_first, shift_second, shift_third])
    sh_a, sh_b, sh_c, sh_d, sh_e, sh_f, sh_g, sh_h, sh_i, sh_j, sh_k = (
        lax.psum_scatter(
            self_in_g.astype(jnp.bfloat16), "narrow", scatter_dimension=0, tiled=True
        ).astype(jnp.float32),
        lax.psum_scatter(
            self_out_g.astype(jnp.bfloat16), "narrow", scatter_dimension=0, tiled=True
        ).astype(jnp.float32),
        lax.psum_scatter(
            cross_q_g.astype(jnp.bfloat16), "narrow", scatter_dimension=0, tiled=True
        ).astype(jnp.float32),
        lax.psum_scatter(
            cross_kv_g.astype(jnp.bfloat16), "narrow", scatter_dimension=0, tiled=True
        ).astype(jnp.float32),
        lax.psum_scatter(
            cross_out_g.astype(jnp.bfloat16), "narrow", scatter_dimension=0, tiled=True
        ).astype(jnp.float32),
        lax.psum_scatter(
            ffn_in_g.astype(jnp.bfloat16), "narrow", scatter_dimension=0, tiled=True
        ).astype(jnp.float32),
        lax.psum_scatter(
            ffn_in_bias_g.astype(jnp.bfloat16), "narrow", scatter_dimension=0, tiled=True
        ).astype(jnp.float32),
        lax.psum_scatter(
            ffn_out_g.astype(jnp.bfloat16), "narrow", scatter_dimension=0, tiled=True
        ).astype(jnp.float32),
        lax.psum_scatter(
            ffn_out_bias_g.astype(jnp.bfloat16), "narrow", scatter_dimension=0, tiled=True
        ).astype(jnp.float32),
        lax.psum_scatter(
            gain_g.astype(jnp.bfloat16), "narrow", scatter_dimension=1, tiled=True
        ).astype(jnp.float32),
        lax.psum_scatter(
            shift_g.astype(jnp.bfloat16), "narrow", scatter_dimension=1, tiled=True
        ).astype(jnp.float32),
    )
    summed = (
        lax.psum(sh_a.astype(jnp.bfloat16), "wide").astype(jnp.float32),
        lax.psum(sh_b.astype(jnp.bfloat16), "wide").astype(jnp.float32),
        lax.psum(sh_c.astype(jnp.bfloat16), "wide").astype(jnp.float32),
        lax.psum(sh_d.astype(jnp.bfloat16), "wide").astype(jnp.float32),
        lax.psum(sh_e.astype(jnp.bfloat16), "wide").astype(jnp.float32),
        lax.psum(sh_f.astype(jnp.bfloat16), "wide").astype(jnp.float32),
        lax.psum(sh_g.astype(jnp.bfloat16), "wide").astype(jnp.float32),
        lax.psum(sh_h.astype(jnp.bfloat16), "wide").astype(jnp.float32),
        lax.psum(sh_i.astype(jnp.bfloat16), "wide").astype(jnp.float32),
        lax.psum(sh_j.astype(jnp.bfloat16), "wide").astype(jnp.float32),
        lax.psum(sh_k.astype(jnp.bfloat16), "wide").astype(jnp.float32),
    )
    return (
        result.astype(jnp.bfloat16),
        target_grad,
        memory_grad,
        summed[0],
        summed[1],
        summed[2],
        summed[3],
        summed[4],
        summed[5],
        summed[6],
        summed[7],
        summed[8],
        summed[9],
        summed[10],
    )


def solution(mesh):
    in_specs = (
        P("wide", "narrow", None),
        P("wide", "narrow", None),
        P("wide", None),
        P("wide", None),
        P(),
        P(),
        P(),
        P(),
        P(),
        P(),
        P(),
        P(),
        P(),
        P(),
        P(),
        P("wide", "narrow", None),
    )
    out_specs = (
        P("wide", "narrow", None),
        P("wide", "narrow", None),
        P("wide", "narrow", None),
        P("narrow", None),
        P("narrow", None),
        P("narrow", None),
        P("narrow", None),
        P("narrow", None),
        P("narrow", None),
        P("narrow"),
        P("narrow", None),
        P("narrow"),
        P(None, "narrow"),
        P(None, "narrow"),
    )
    return jax.shard_map(local, mesh=mesh, in_specs=in_specs, out_specs=out_specs, check_vma=False)
```

profile of v0, /device:TPU:0, one launch (start us, length us, event | category | flops | bytes accessed | tf_op | source)
XLA Modules:
  0.0 479.6 jit_solution(14158876965380857701)
XLA Ops:
  7.3 2.7 convolution_convert_fusion.5
  10.1 2.0 fusion.5
  15.8 18.4 %all-gather.6.cloned.1.call-done = bf16[512,1024]{1,0:T(8,128)(2,1)} async-done(((bf16[256,1024]{1,0:T(8,128)(2,1)}), bf16[512,1024]{1,0:T(8,128)(2,1)}) %all-gather.6.cloned.1.call-update) | async-done | bytes 1048592 | tf_op jit(solution)/shard_map/all_gather | solution.py:230
  34.2 2.1 fusion.65
  36.3 2.0 copy.79
  38.3 1.0 copy.77
  39.3 18.3 %all-gather.4.cloned.1.call-done = bf16[1,512,1024]{2,1,0:T(8,128)(2,1)} async-done(((bf16[1,256,1024]{2,1,0:T(8,128)(2,1)}), bf16[1,512,1024]{2,1,0:T(8,128)(2,1)}) %all-gather.4.cloned.1.call-update) | async-done | bytes 1048592 | tf_op jit(solution)/shard_map/all_gather | solution.py:207
  57.7 2.2 fusion.66
  59.9 1.3 copy.76
  61.2 2.2 copy.74
  63.4 0.9 fusion.3
  64.3 1.3 exponential_reduce_fusion.1
  66.3 2.0 fusion.69
  69.7 1.1 convolution_convert_fusion.17
  70.8 1.8 copy.78
  72.6 1.9 fusion.4
  74.6 1.3 exponential_reduce_fusion
  76.6 2.0 fusion.71
  79.3 1.0 copy-done.22
  81.1 0.9 fusion.73
  83.1 1.0 fusion.64
  84.1 2.6 fusion.74
  86.7 1.5 multiply_reduce_fusion
  89.4 3.5 convolution_convert_fusion.9
  93.2 2.8 multiply_convert_fusion.1
  95.9 1.5 convolution_convert_fusion.15
  97.9 1.0 pad_maximum_fusion.1
  99.6 1.0 multiply_reduce_fusion.1
  102.2 1.1 multiply_reduce_fusion.2
  103.4 4.6 multiply_convert_fusion
  109.0 1.2 convolution_convert_fusion.11
  110.2 1.0 pad_maximum_fusion
  111.4 2.3 convolution_convert_fusion.6
  113.7 2.2 convolution_convert_fusion.7
  116.1 2.4 convolution_convert_fusion.8
  118.7 4.0 convolution_convert_fusion
  123.4 3.4 convolution_convert_fusion.1
  126.9 2.6 fusion.12
  129.6 1.5 convolution_convert_fusion.13
  131.1 11.5 %reduce-scatter.16.cloned.1.call-done = bf16[1,256,1024]{1,2,0:T(8,128)(2,1)} async-done(((bf16[1,512,1024]{1,2,0:T(8,128)(2,1)}), bf16[1,256,1024]{1,2,0:T(8,128)(2,1)}) %reduce-scatter.16.cloned.1.call-update) | async-done | bytes 524304 | tf_op jit(solution)/shard_map/reduce_scatter | solution.py:298
  142.6 2.9 fusion.2
  147.6 12.3 %reduce-scatter.28.cloned.1.call-done = bf16[256,512]{1,0:T(8,128)(2,1)} async-done(((bf16[512,512]{1,0:T(8,128)(2,1)}), bf16[256,512]{1,0:T(8,128)(2,1)}) %reduce-scatter.28.cloned.1.call-update) | async-done | bytes 262160 | tf_op jit(solution)/shard_map/reduce_scatter | solution.py:319
  159.9 17.3 %reduce-scatter.24.cloned.1.call-done = bf16[256,512]{1,0:T(8,128)(2,1)} async-done(((bf16[512,512]{1,0:T(8,128)(2,1)}), bf16[256,512]{1,0:T(8,128)(2,1)}) %reduce-scatter.24.cloned.1.call-update) | async-done | bytes 262160 | tf_op jit(solution)/shard_map/reduce_scatter | solution.py:313
  177.2 17.4 %reduce-scatter.22.cloned.1.call-done = bf16[256,512]{1,0:T(8,128)(2,1)} async-done(((bf16[512,512]{1,0:T(8,128)(2,1)}), bf16[256,512]{1,0:T(8,128)(2,1)}) %reduce-scatter.22.cloned.1.call-update) | async-done | bytes 262160 | tf_op jit(solution)/shard_map/reduce_scatter | solution.py:310
  194.6 34.8 %reduce-scatter.32.cloned.1.call-done = bf16[1024,512]{1,0:T(8,128)(2,1)} async-done(((bf16[2048,512]{1,0:T(8,128)(2,1)}), bf16[1024,512]{1,0:T(8,128)(2,1)}) %reduce-scatter.32.cloned.1.call-update) | async-done | bytes 1048592 | tf_op jit(solution)/shard_map/reduce_scatter | solution.py:328
  229.4 34.7 %reduce-scatter.30.cloned.1.call-done = bf16[256,2048]{1,0:T(8,128)(2,1)} async-done(((bf16[512,2048]{1,0:T(8,128)(2,1)}), bf16[256,2048]{1,0:T(8,128)(2,1)}) %reduce-scatter.30.cloned.1.call-update) | async-done | bytes 1048592 | tf_op jit(solution)/shard_map/reduce_scatter | solution.py:322
  264.1 22.5 %reduce-scatter.26.cloned.1.call-done = bf16[256,1024]{0,1:T(8,128)(2,1)} async-done(((bf16[512,1024]{0,1:T(8,128)(2,1)}), bf16[256,1024]{0,1:T(8,128)(2,1)}) %reduce-scatter.26.cloned.1.call-update) | async-done | bytes 524304 | tf_op jit(solution)/shard_map/reduce_scatter | solution.py:316
  286.6 28.9 %reduce-scatter.20.cloned.1.call-done = bf16[256,1536]{0,1:T(8,128)(2,1)} async-done(((bf16[512,1536]{0,1:T(8,128)(2,1)}), bf16[256,1536]{0,1:T(8,128)(2,1)}) %reduce-scatter.20.cloned.1.call-update) | async-done | bytes 786448 | tf_op jit(solution)/shard_map/reduce_scatter | solution.py:307
  318.2 5.0 %all-reduce.4 = (bf16[2048]{0:T(1024)(128)(2,1)S(1)}, bf16[512]{0:T(512)(128)(2,1)S(1)}) all-reduce(bf16[2048]{0:T(1024)(128)(2,1)S(1)} %copy-done.81, bf16[512]{0:T(512)(128)(2,1)S(1)} %add_reduce_fusion), channel_id=11, replica_groups=mesh['wide'=16,'narrow'=2] {'narrow'}, use_global_device_ids=true, to_apply=%region_37.38.clone | all-reduce | flops 2560 | bytes 10240
  323.3 4.7 reduce-scatter.36.cloned.1.call-done
  328.0 0.9 copy.89
  328.9 12.2 %reduce-scatter.34.cloned.1.call-done = bf16[256,3]{1,0:T(8,128)(2,1)} async-done(((bf16[512,3]{1,0:T(8,128)(2,1)}), bf16[256,3]{1,0:T(8,128)(2,1)}) %reduce-scatter.34.cloned.1.call-update) | async-done | bytes 1552
  341.1 0.9 copy.87
  342.0 34.9 %all-reduce.2 = (bf16[1024]{0:T(1024)(128)(2,1)S(1)}, bf16[256]{0:T(256)(128)(2,1)S(1)}, bf16[3,256]{1,0:T(4,128)(2,1)S(1)}, bf16[3,256]{1,0:T(4,128)(2,1)S(1)}) all-reduce(bf16[1024]{0:T(1024)(128)(2,1)S(1)} %dynamic-slice.2, bf16[256]{0:T(256)(128)(2,1)S(1)} %dynamic-slice.4, ...), channel_id=1, replica_groups=mesh['wide'=16,'narrow'=2] {'wide'}, use_global_device_ids=true, to_apply=%region_38.39 | all-reduce | flops 2816 | bytes 11264 | tf_op jit(solution)/shard_map/psum | solution.py:348
  379.3 1.3 convolution_bitcast_fusion
  380.6 2.5 fusion.13
  383.0 77.3 %all-reduce.7.cloned.1.call-done = (bf16[256,1536]{0,1:T(8,128)(2,1)}, bf16[256,1024]{0,1:T(8,128)(2,1)}, bf16[256,512]{1,0:T(8,128)(2,1)}, bf16[256,512]{1,0:T(...) async-done(((bf16[256,1536]{0,1:T(8,128)(2,1)}, bf16[256,1024]{0,1:T(8,128)(2,1)}, bf16[256,512]{1,0:T(8,128)(2,1)}, ...) | async-done | bytes 4194320 | tf_op jit(solution)/shard_map/psum | solution.py:342
  460.3 1.9 convert_element_type.326
  462.2 1.9 convert_element_type.328
  464.1 1.8 convert_element_type.333
  465.9 1.4 copy.84
  467.3 1.2 copy.85
  468.5 2.9 convert_element_type.335
  471.4 1.6 convert_element_type.339
  (268 shorter events, 21.0 us)
Async XLA Ops:
  7.2 73.9 %copy-start = (bf16[2048,512]{1,0:T(8,128)(2,1)S(1)}, bf16[2048,512]{1,0:T(8,128)(2,1)}, u32[]{:S(2)}) copy-start(bf16[2048,512]{1,0:T(8,128)(2,1)} %param.27) | copy-start | bytes 6291460
  7.2 2.9 copy-start.15
  7.2 27.0 %all-gather.6.cloned.1.call-start = ((), (), s32[]{:S(2)}) async-start(), calls=%async_computation.21 | async-start | bytes 1572864 | tf_op jit(solution)/shard_map/all_gather | solution.py:230
  10.0 3.1 copy-start.85
  10.0 3.3 copy-start.86
  10.0 3.7 copy-start.74
  10.0 4.3 copy-start.75
  10.0 47.6 %all-gather.4.cloned.1.call-start = ((), (), s32[]{:S(2)}) async-start(), calls=%async_computation.11 | async-start | bytes 1572864 | tf_op jit(solution)/shard_map/all_gather | solution.py:207
  13.0 114.0 %reduce-scatter.18.cloned.1.call-start = ((), (), s32[]{:S(2)}) async-start(), calls=%async_computation.13 | async-start | bytes 1572864 | tf_op jit(solution)/shard_map/reduce_scatter | solution.py:273
  13.6 49.8 %copy-start.19 = (bf16[1,256,512]{1,2,0:T(8,128)(2,1)}, bf16[1,256,512]{1,2,0:T(8,128)(2,1)S(1)}, u32[]{:S(2)}) copy-start(bf16[1,256,512]{1,2,0:T(8,128)(2,1)S(1)} %copy.75) | copy-start | bytes 786436
  61.1 3.2 copy-start.10
  65.7 2.6 copy-start.69
  68.3 4.3 copy-start.12
  69.7 8.9 %copy-start.51 = (f32[256]{0:T(256)}, f32[256]{0:T(256)S(1)}, u32[]{:S(2)}) copy-start(f32[256]{0:T(256)S(1)} %fusion.40) | copy-start | bytes 3076
  75.9 2.7 copy-start.71
  79.2 9.0 %copy-start.49 = (f32[256]{0:T(256)}, f32[256]{0:T(256)S(1)}, u32[]{:S(2)}) copy-start(f32[256]{0:T(256)S(1)} %fusion.41) | copy-start | bytes 3076
  81.1 3.0 copy-start.23
  84.1 2.6 copy-start.24
  84.1 2.6 copy-start.79
  88.5 4.4 copy-start.6
  89.2 3.7 copy-start.48
  89.4 3.6 copy-start.46
  89.4 3.7 copy-start.5
  89.4 3.7 copy-start.35
  89.4 3.7 copy-start.45
  89.4 3.7 copy-start.73
  93.2 2.8 copy-start.13
  99.0 43.6 %reduce-scatter.16.cloned.1.call-start = ((), (), s32[]{:S(2)}) async-start(), calls=%async_computation.12 | async-start | bytes 1572864 | tf_op jit(solution)/shard_map/reduce_scatter | solution.py:298
  100.9 2.5 copy-start.8
  100.9 2.5 copy-start.66
  103.4 4.6 copy-start.20
  103.4 5.1 %copy-start.3 = (f32[8,256,512]{2,1,0:T(8,128)S(1)}, f32[8,256,512]{2,1,0:T(8,128)}, u32[]{:S(2)}) copy-start(f32[8,256,512]{2,1,0:T(8,128)} %copy-done.2) | copy-start | bytes 12582916
  110.2 3.5 copy-start.53
  110.2 3.5 copy-start.59
  111.3 4.8 copy-start.67
  111.3 48.5 %reduce-scatter.28.cloned.1.call-start = ((), (), s32[]{:S(2)}) async-start(), calls=%async_computation.18 | async-start | bytes 786432 | tf_op jit(solution)/shard_map/reduce_scatter | solution.py:319
  113.7 5.1 %copy-start.80 = (f32[256]{0:T(256)S(1)}, f32[256]{0:T(256)}, u32[]{:S(2)}) copy-start(f32[256]{0:T(256)} %copy-done.79) | copy-start | bytes 3076
  113.7 63.5 %reduce-scatter.24.cloned.1.call-start = ((), (), s32[]{:S(2)}) async-start(), calls=%async_computation.16 | async-start | bytes 786432 | tf_op jit(solution)/shard_map/reduce_scatter | solution.py:313
  116.0 2.7 copy-start.25
  116.0 78.6 %reduce-scatter.22.cloned.1.call-start = ((), (), s32[]{:S(2)}) async-start(), calls=%async_computation.15 | async-start | bytes 786432 | tf_op jit(solution)/shard_map/reduce_scatter | solution.py:310
  118.4 110.9 %reduce-scatter.32.cloned.1.call-start = ((), (), s32[]{:S(2)}) async-start(), calls=%async_computation.20 | async-start | bytes 3145728 | tf_op jit(solution)/shard_map/reduce_scatter | solution.py:328
  122.8 141.3 %reduce-scatter.30.cloned.1.call-start = ((), (), s32[]{:S(2)}) async-start(), calls=%async_computation.19 | async-start | bytes 3145728 | tf_op jit(solution)/shard_map/reduce_scatter | solution.py:322
  126.8 2.8 copy-start.11
  126.9 159.7 %reduce-scatter.26.cloned.1.call-start = ((), (), s32[]{:S(2)}) async-start(), calls=%async_computation.17 | async-start | bytes 1572864 | tf_op jit(solution)/shard_map/reduce_scatter | solution.py:316
  129.5 185.9 %reduce-scatter.20.cloned.1.call-start = ((), (), s32[]{:S(2)}) async-start(), calls=%async_computation.14 | async-start | bytes 2359296 | tf_op jit(solution)/shard_map/reduce_scatter | solution.py:307
  142.6 3.0 copy-start.17
  142.6 3.0 copy-start.76
  142.6 3.1 copy-start.83
  142.6 3.1 copy-start.82
  142.6 3.1 copy-start.78
  142.6 3.1 copy-start.77
  145.5 182.5 %reduce-scatter.36.cloned.1.call-start = ((), (), s32[]{:S(2)}) async-start(), calls=%async_computation.23 | async-start | bytes 196608
  146.6 194.5 %reduce-scatter.34.cloned.1.call-start = ((), (), s32[]{:S(2)}) async-start(), calls=%async_computation.22 | async-start | bytes 196608
  147.5 312.8 %all-reduce.7.cloned.1.call-start = ((), (), s32[]{:S(2)}) async-start(), calls=%async_computation.24 | async-start | bytes 8388608 | tf_op jit(solution)/shard_map/psum | solution.py:342
  315.5 2.7 copy-start.81
  315.5 63.8 %copy-start.14 = (bf16[512,1024]{1,0:T(8,128)(2,1)S(1)}, bf16[512,1024]{1,0:T(8,128)(2,1)}, u32[]{:S(2)}) copy-start(bf16[512,1024]{1,0:T(8,128)(2,1)} %param.23) | copy-start | bytes 3145732
  315.5 63.8 %copy-start.28 = (bf16[1,256,1024]{1,2,0:T(8,128)(2,1)S(1)}, bf16[1,256,1024]{1,2,0:T(8,128)(2,1)}, u32[]{:S(2)}) copy-start(bf16[1,256,1024]{1,2,0:T(8,128)(2,1)} %reduce-scatter.18.cloned.1.call-done) | copy-start | bytes 1572868
  315.5 65.0 %copy-start.9 = (f32[1,256,512]{2,1,0:T(8,128)S(1)}, f32[1,256,512]{2,1,0:T(8,128)}, u32[]{:S(2)}) copy-start(f32[1,256,512]{2,1,0:T(8,128)} %copy-done.8) | copy-start | bytes 1572868
  315.5 65.0 %copy-start.39 = (bf16[8,64,256]{2,1,0:T(8,128)(2,1)S(1)}, bf16[8,64,256]{2,1,0:T(8,128)(2,1)}, u32[]{:S(2)}) copy-start(bf16[8,64,256]{2,1,0:T(8,128)(2,1)} %convolution_convert_fusion.13) | copy-start | bytes 786436
  376.9 3.7 copy-start.32
  460.3 5.5 %copy-start.41 = (bf16[256,1536]{0,1:T(8,128)(2,1)S(1)}, bf16[256,1536]{0,1:T(8,128)(2,1)}, u32[]{:S(2)}) copy-start(bf16[256,1536]{0,1:T(8,128)(2,1)} %get-tuple-element.196) | copy-start | bytes 2359300
  462.2 5.1 %copy-start.42 = (bf16[256,1024]{0,1:T(8,128)(2,1)S(1)}, bf16[256,1024]{0,1:T(8,128)(2,1)}, u32[]{:S(2)}) copy-start(bf16[256,1024]{0,1:T(8,128)(2,1)} %get-tuple-element.197) | copy-start | bytes 1572868
  467.3 4.1 copy-start.36
  468.5 4.6 copy-start.1
  (38 other events, 52.8 us)
Sparse Core Ops, SparseCore 0:
  10.2 23.9 all-gather.5
  36.3 21.2 all-gather.3
  99.1 20.3 reduce-scatter.17
  122.2 20.3 reduce-scatter.15
  145.3 14.5 reduce-scatter.27
  162.6 14.5 reduce-scatter.23
  180.0 14.5 reduce-scatter.21
  197.5 31.8 reduce-scatter.31
  232.2 31.8 reduce-scatter.29
  266.2 20.3 reduce-scatter.25
  289.4 26.0 reduce-scatter.19
  317.6 10.2 reduce-scatter.35
  330.8 10.2 reduce-scatter.33
  346.3 114.0 all-reduce.6
where the time goes:
time: 481 us; the launch traced here: 480 us
  waiting for transfers between devices  311 us (65%)
  matrix products  60.3 us (13%)
  blocking collectives  39.9 us (8%)
  local copies, waits for them, and re-layouts  28.6 us (6%)
  other arithmetic  22.9 us (5%)
  between operations  16.3 us (3%)
    psum x1, waiting for transfers between devices, local(): lax.psum(sh_a.astype(jnp.bfloat16), 'wide').astype(jnp.float32)  77.3 us
    psum x1, blocking collectives, local(): lax.psum(sh_g.astype(jnp.bfloat16), 'wide').astype(jnp.float32)  34.9 us
    reduce_scatter x1, waiting for transfers between devices, local(): lax.psum_scatter(ffn_out_g.astype(jnp.bfloat16), 'narrow', scatter_dimens...  34.8 us
    reduce_scatter x1, waiting for transfers between devices, local(): lax.psum_scatter(ffn_in_g.astype(jnp.bfloat16), 'narrow', scatter_dimensi...  34.7 us
    reduce_scatter x1, waiting for transfers between devices, local(): lax.psum_scatter(self_in_g.astype(jnp.bfloat16), 'narrow', scatter_dimens...  28.9 us
    reduce_scatter x1, waiting for transfers between devices, local(): lax.psum_scatter(cross_kv_g.astype(jnp.bfloat16), 'narrow', scatter_dimen...  22.5 us
    dot_general x7, matrix products, weight_grad(): jnp.einsum('rsd,rse->de', activity, gradient, preferred_element_type=jnp....  19.7 us
    all_gather x1, waiting for transfers between devices, local(): lax.all_gather(cross_pairs, 'narrow', axis=1, tiled=True)  18.4 us
  transfers between devices with their start and end apart: 14, of which 13 were waited for; matrix products, arithmetic and copies ran while one was open for 11% of the time, Pallas kernels for 0%

commit v1 on v0

--- a/solution.py
+++ b/solution.py
@@ -3,6 +3,8 @@
 import jax
 import jax.numpy as jnp
 from jax import lax
+from jax.experimental import pallas as pl
+from jax.experimental.pallas import tpu as pltpu
 from jax.sharding import PartitionSpec as P
 
 HEADS = 8
@@ -369,6 +371,521 @@
     )
 
 
+def dot_nn(left, right):
+    return jnp.dot(left, right, preferred_element_type=jnp.float32)
+
+
+def dot_nt(left, right):
+    return lax.dot_general(left, right, (((1,), (1,)), ((), ())), preferred_element_type=jnp.float32)
+
+
+def dot_tn(left, right):
+    return lax.dot_general(left, right, (((0,), (0,)), ((), ())), preferred_element_type=jnp.float32)
+
+
+def low(values):
+    return values.astype(jnp.bfloat16)
+
+
+def normalize(values):
+    centre = values - jnp.mean(values, axis=-1, keepdims=True)
+    scale = lax.rsqrt(jnp.mean(centre * centre, axis=-1, keepdims=True) + EPSILON)
+    return centre * scale, scale
+
+
+def normalize_back(grad, gain, unit, scale):
+    inner = grad * gain
+    return scale * (
+        inner
+        - jnp.mean(inner, axis=-1, keepdims=True)
+        - unit * jnp.mean(inner * unit, axis=-1, keepdims=True)
+    )
+
+
+def seg_along(lens_ref, shape, dim):
+    places = lax.broadcasted_iota(jnp.int32, shape, dim)
+    seg = jnp.zeros(shape, jnp.int32)
+    end = jnp.int32(0)
+    for doc in range(lens_ref.shape[1]):
+        end = end + lens_ref[0, doc]
+        seg = seg + (places >= end).astype(jnp.int32)
+    return seg
+
+
+def visible_pairs(query_lens, key_lens, length, causal):
+    seen = seg_along(query_lens, (length, 1), 0) == seg_along(key_lens, (1, length), 1)
+    if causal:
+        rows = lax.broadcasted_iota(jnp.int32, (length, length), 0)
+        cols = lax.broadcasted_iota(jnp.int32, (length, length), 1)
+        seen = seen & (cols <= rows)
+    return seen
+
+
+def join_halves(place_ref, own_ref, other_ref, full_ref):
+    half = own_ref.shape[0]
+    mine = place_ref[0]
+    full_ref[pl.ds(pl.multiple_of(mine * half, half), half), :] = own_ref[...]
+    full_ref[pl.ds(pl.multiple_of((1 - mine) * half, half), half), :] = other_ref[...]
+
+
+def own_columns(ref, start, width):
+    return ref[:, pl.ds(pl.multiple_of(start, 128), width)]
+
+
+def grad_rows(place_ref, activity_ref, grads, keep_ref, send_ref, col):
+    rows = keep_ref.shape[0]
+    first = place_ref[0] * 2 * rows
+    for ref, part in ((keep_ref, place_ref[1]), (send_ref, 1 - place_ref[1])):
+        piece = own_columns(activity_ref, first + part * rows, rows)
+        at = col
+        for grad in grads:
+            ref[:, at : at + grad.shape[1]] = dot_tn(piece, grad).astype(ref.dtype)
+            at += grad.shape[1]
+
+
+def query_blocks(length, causal):
+    if causal:
+        return ((0, length // 2, length // 2), (length // 2, length, length))
+    return ((0, length // 2, length), (length // 2, length, length))
+
+
+PAIR = 2 * HEAD_DIM
+
+
+def head_lanes():
+    lane = lax.broadcasted_iota(jnp.int32, (1, PAIR), 1)
+    return (lane < HEAD_DIM, lane >= HEAD_DIM)
+
+
+def attend_all(query_ref, key_ref, value_ref, bias_ref, attn_ref, mix_ref, causal):
+    length = query_ref.shape[0]
+
+    def one_pair(pair, carry):
+        lanes = pl.ds(pl.multiple_of(pair * PAIR, PAIR), PAIR)
+        keys, values = key_ref[:, lanes], value_ref[:, lanes]
+        zero = jnp.zeros_like(keys)
+        for begin, end, reach in query_blocks(length, causal):
+            queries = query_ref[begin:end, lanes]
+            total = jnp.zeros((end - begin, PAIR), jnp.float32)
+            for sub, inside in enumerate(head_lanes()):
+                scores = dot_nt(queries, jnp.where(inside, keys, zero)[:reach])
+                scores = scores + bias_ref[begin:end, :reach]
+                weights = jnp.exp(scores - jnp.max(scores, axis=-1, keepdims=True))
+                weights = low(weights * (1.0 / jnp.sum(weights, axis=-1, keepdims=True)))
+                attn_ref[pair * 2 + sub, begin:end, :reach] = weights
+                total = total + dot_nn(weights, jnp.where(inside, values, zero)[:reach])
+            mix_ref[begin:end, lanes] = low(total)
+        return carry
+
+    lax.fori_loop(0, HEADS // 2, one_pair, 0)
+
+
+def attend_all_back(
+    query_ref, query_t_ref, key_ref, value_ref, attn_ref, mix_ref, grad_ref, grad_t_ref, dquery_ref, dpairs_t_ref, causal
+):
+    length, width = query_ref.shape
+
+    def one_pair(pair, carry):
+        lanes = pl.ds(pl.multiple_of(pair * PAIR, PAIR), PAIR)
+        keys, values = key_ref[:, lanes], value_ref[:, lanes]
+        zero = jnp.zeros_like(keys)
+        blocks = query_blocks(length, causal)
+        dquery = [jnp.zeros((end - begin, PAIR), jnp.float32) for begin, end, _ in blocks]
+        for sub, inside in enumerate(head_lanes()):
+            head_keys = jnp.where(inside, keys, zero)
+            head_values = jnp.where(inside, values, zero)
+            rows = pl.ds(pl.multiple_of(pair * PAIR + sub * HEAD_DIM, HEAD_DIM), HEAD_DIM)
+            parts = []
+            for idx, (begin, end, reach) in enumerate(blocks):
+                grads = grad_ref[begin:end, lanes]
+                dots = grads.astype(jnp.float32) * mix_ref[begin:end, lanes].astype(jnp.float32)
+                row_dot = jnp.sum(jnp.where(inside, dots, 0.0), axis=-1, keepdims=True)
+                weights = attn_ref[pair * 2 + sub, begin:end, :reach]
+                dattn = dot_nt(grads, head_values[:reach])
+                dscores = low(weights.astype(jnp.float32) * (dattn - row_dot))
+                dquery[idx] = dquery[idx] + dot_nn(dscores, head_keys[:reach])
+                dkey_t = dot_nn(query_t_ref[rows, begin:end], dscores)
+                dvalue_t = dot_nn(grad_t_ref[rows, begin:end], weights)
+                parts.append((reach, dkey_t, dvalue_t))
+            (reach, dkey_t, dvalue_t), (_, dkey_more, dvalue_more) = parts
+            rows_v = pl.ds(pl.multiple_of(width + pair * PAIR + sub * HEAD_DIM, HEAD_DIM), HEAD_DIM)
+            for where, less, more in ((rows, dkey_t, dkey_more), (rows_v, dvalue_t, dvalue_more)):
+                dpairs_t_ref[where, :reach] = low(less + more[:, :reach])
+                if reach < length:
+                    dpairs_t_ref[where, reach:] = low(more[:, reach:])
+        for (begin, end, _), dq in zip(blocks, dquery):
+            dquery_ref[begin:end, lanes] = low(dq * HEAD_DIM ** (-0.5))
+        return carry
+
+    lax.fori_loop(0, HEADS // 2, one_pair, 0)
+
+
+def self_forward_kernel(
+    place_ref, lens_ref, own_ref, other_ref, self_in_ref, self_out_ref,
+    triple_ref, attn_ref, mix_ref, unit_ref, scale_ref,
+    full_ref, bias_ref,
+):
+    length, width = full_ref.shape
+    join_halves(place_ref, own_ref, other_ref, full_ref)
+    bias_ref[...] = jnp.where(visible_pairs(lens_ref, lens_ref, length, True), 0.0, MASKED)
+    triple_ref[:, :width] = low(
+        low(dot_nn(full_ref[...], self_in_ref[:, :width])) * jnp.bfloat16(HEAD_DIM ** (-0.5))
+    )
+    triple_ref[:, width:] = low(dot_nn(full_ref[...], self_in_ref[:, width:]))
+    attend_all(
+        triple_ref.at[:, :width],
+        triple_ref.at[:, width : 2 * width],
+        triple_ref.at[:, 2 * width :],
+        bias_ref,
+        attn_ref,
+        mix_ref,
+        True,
+    )
+    summed = full_ref[...].astype(jnp.float32) + dot_nn(mix_ref[...], self_out_ref[...])
+    unit_ref[...], scale_ref[...] = normalize(summed)
+
+
+def cross_forward_kernel(
+    place_ref, target_lens_ref, source_lens_ref, own_ref, other_ref, unit_first_ref,
+    cross_q_ref, cross_kv_ref, cross_out_ref, gain_ref, shift_ref,
+    query_ref, pairs_ref, attn_ref, mix_ref, unit_ref, scale_ref,
+    full_ref, bias_ref,
+):
+    length, width = full_ref.shape
+    join_halves(place_ref, own_ref, other_ref, full_ref)
+    bias_ref[...] = jnp.where(visible_pairs(target_lens_ref, source_lens_ref, length, False), 0.0, MASKED)
+    first = unit_first_ref[...] * gain_ref[0:1, :] + shift_ref[0:1, :]
+    query_ref[...] = low(low(dot_nn(low(first), cross_q_ref[...])) * jnp.bfloat16(HEAD_DIM ** (-0.5)))
+    pairs_ref[...] = low(dot_nn(full_ref[...], cross_kv_ref[...]))
+    attend_all(
+        query_ref, pairs_ref.at[:, :width], pairs_ref.at[:, width:], bias_ref, attn_ref, mix_ref, False
+    )
+    first = unit_first_ref[...] * gain_ref[0:1, :] + shift_ref[0:1, :]
+    unit_ref[...], scale_ref[...] = normalize(first + dot_nn(mix_ref[...], cross_out_ref[...]))
+
+
+GELU_SCALE = math.sqrt(2.0 / math.pi)
+GELU_CUBE = 0.044715
+
+
+def gelu_both(values):
+    square = values * values
+    bent = jnp.tanh(GELU_SCALE * (values + GELU_CUBE * (square * values)))
+    half_up = 0.5 * (1.0 + bent)
+    slope = half_up + 0.5 * values * (1.0 - bent * bent) * (
+        GELU_SCALE * (1.0 + 3.0 * GELU_CUBE * square)
+    )
+    return values * half_up, slope
+
+
+def feed_kernel(
+    place_ref, own_ref, other_ref, unit_second_ref, scale_second_ref,
+    ffn_in_ref, ffn_in_bias_ref, ffn_out_ref, ffn_out_bias_ref, gain_ref, shift_ref,
+    output_ref, out_keep_ref, out_send_ref, in_keep_ref, in_send_ref,
+    in_bias_grad_ref, norm_grad_ref, grad_second_ref,
+    full_ref, second_ref, active_ref, slope_ref, outer_ref, inner_ref,
+):
+    length, width = full_ref.shape
+    half = length // 2
+    hidden = ffn_in_ref.shape[1]
+    block = min(hidden, 512)
+    join_halves(place_ref, own_ref, other_ref, full_ref)
+    second = unit_second_ref[...] * gain_ref[1:2, :] + shift_ref[1:2, :]
+    second_ref[...] = low(second)
+    total = second + ffn_out_bias_ref[...]
+    for begin in range(0, hidden, block):
+        cols = slice(begin, begin + block)
+        inner = dot_nn(second_ref[...], ffn_in_ref[:, cols]) + ffn_in_bias_ref[:, cols]
+        active, slope_ref[:, cols] = gelu_both(inner)
+        active_ref[:, cols] = low(active)
+        total = total + dot_nn(active_ref[:, cols], ffn_out_ref[cols, :])
+    unit, scale = normalize(total)
+    shown = unit * gain_ref[2:3, :] + shift_ref[2:3, :]
+    cotangent = full_ref[...].astype(jnp.float32)
+    norm_grad_ref[0:1, :] = jnp.sum(cotangent * unit, axis=0, keepdims=True)
+    norm_grad_ref[1:2, :] = jnp.sum(cotangent, axis=0, keepdims=True)
+    grad_third = normalize_back(cotangent, gain_ref[2:3, :], unit, scale)
+    norm_grad_ref[4:5, :] = jnp.sum(grad_third, axis=0, keepdims=True)
+    outer_ref[...] = low(grad_third)
+    grad_second_ref[...] = shown
+    output_ref[...] = low(
+        grad_second_ref[pl.ds(pl.multiple_of(place_ref[0] * half, half), half), :]
+    )
+    grad_second_ref[...] = grad_third
+    grad_rows(place_ref, active_ref, (outer_ref[...],), out_keep_ref, out_send_ref, 0)
+    into_second = jnp.zeros((length, width), jnp.float32)
+    for begin in range(0, hidden, block):
+        cols = slice(begin, begin + block)
+        grad_inner = dot_nt(outer_ref[...], ffn_out_ref[cols, :]) * slope_ref[:, cols]
+        in_bias_grad_ref[:, cols] = jnp.sum(grad_inner, axis=0, keepdims=True)
+        inner_ref[:, cols] = low(grad_inner)
+        into_second = into_second + dot_nt(inner_ref[:, cols], ffn_in_ref[:, cols])
+    grad_rows(place_ref, second_ref, (inner_ref[...],), in_keep_ref, in_send_ref, 0)
+    grad = grad_second_ref[...] + into_second
+    unit_second = unit_second_ref[...]
+    norm_grad_ref[2:3, :] = jnp.sum(grad * unit_second, axis=0, keepdims=True)
+    norm_grad_ref[3:4, :] = jnp.sum(grad, axis=0, keepdims=True)
+    norm_grad_ref[5:8, :] = jnp.zeros((3, width), jnp.float32)
+    grad_second_ref[...] = normalize_back(grad, gain_ref[1:2, :], unit_second, scale_second_ref[...])
+
+
+def cross_back_kernel(
+    place_ref, target_lens_ref, source_lens_ref, own_ref, other_ref, grad_second_ref, unit_first_ref, scale_first_ref,
+    query_ref, pairs_ref, attn_ref, mix_ref, cross_q_ref, cross_kv_ref, cross_out_ref, gain_ref, shift_ref,
+    keep_ref, send_ref, memory_grad_ref, norm_grad_ref, grad_first_ref,
+    full_ref, first_ref, grad_ref, dmix_ref, dmix_t_ref, query_t_ref, dquery_ref, dpairs_t_ref,
+):
+    length, width = full_ref.shape
+    half = length // 2
+    join_halves(place_ref, own_ref, other_ref, full_ref)
+    first_ref[...] = low(unit_first_ref[...] * gain_ref[0:1, :] + shift_ref[0:1, :])
+    grad_ref[...] = low(grad_second_ref[...])
+    seen = jnp.where(visible_pairs(target_lens_ref, source_lens_ref, length, False), 1.0, 0.0)
+    dmix_ref[...] = low(
+        dot_nt(grad_ref[...], cross_out_ref[...]) * jnp.max(seen, axis=-1, keepdims=True)
+    )
+    dmix_t_ref[...] = low(dot_nt(cross_out_ref[...], grad_ref[...]))
+    query_t_ref[...] = query_ref[...].T
+    attend_all_back(
+        query_ref, query_t_ref, pairs_ref.at[:, :width], pairs_ref.at[:, width:], attn_ref, mix_ref,
+        dmix_ref, dmix_t_ref, dquery_ref, dpairs_t_ref, False,
+    )
+    dpairs = dpairs_t_ref[...].T
+    grad_rows(place_ref, first_ref, (dquery_ref[...],), keep_ref, send_ref, 0)
+    grad_rows(place_ref, full_ref, (dpairs,), keep_ref, send_ref, width)
+    grad_rows(place_ref, mix_ref, (grad_ref[...],), keep_ref, send_ref, 3 * width)
+    own_dpairs = own_columns(dpairs_t_ref, place_ref[0] * half, half).T
+    memory_grad_ref[...] = dot_nt(own_dpairs, cross_kv_ref[...])
+    grad = grad_second_ref[...] + dot_nt(dquery_ref[...], cross_q_ref[...])
+    unit_first = unit_first_ref[...]
+    norm_grad_ref[0:1, :] = jnp.sum(grad * unit_first, axis=0, keepdims=True)
+    norm_grad_ref[1:2, :] = jnp.sum(grad, axis=0, keepdims=True)
+    norm_grad_ref[2:8, :] = jnp.zeros((6, width), jnp.float32)
+    grad_first_ref[...] = normalize_back(grad, gain_ref[0:1, :], unit_first, scale_first_ref[...])
+
+
+def self_back_kernel(
+    place_ref, own_ref, other_ref, grad_first_ref, triple_ref, attn_ref, mix_ref, self_in_ref, self_out_ref,
+    keep_ref, send_ref, target_grad_ref,
+    full_ref, grad_ref, dmix_ref, dmix_t_ref, query_t_ref, dquery_ref, dpairs_t_ref,
+):
+    length, width = full_ref.shape
+    half = length // 2
+    join_halves(place_ref, own_ref, other_ref, full_ref)
+    grad_ref[...] = low(grad_first_ref[...])
+    dmix_ref[...] = low(dot_nt(grad_ref[...], self_out_ref[...]))
+    dmix_t_ref[...] = low(dot_nt(self_out_ref[...], grad_ref[...]))
+    query_t_ref[...] = triple_ref[:, :width].T
+    attend_all_back(
+        triple_ref.at[:, :width], query_t_ref, triple_ref.at[:, width : 2 * width], triple_ref.at[:, 2 * width :],
+        attn_ref, mix_ref, dmix_ref, dmix_t_ref, dquery_ref, dpairs_t_ref, True,
+    )
+    dpairs = dpairs_t_ref[...].T
+    grad_rows(place_ref, full_ref, (dquery_ref[...], dpairs), keep_ref, send_ref, 0)
+    grad_rows(place_ref, mix_ref, (grad_ref[...],), keep_ref, send_ref, 3 * width)
+    own_rows = pl.ds(pl.multiple_of(place_ref[0] * half, half), half)
+    own_dpairs = own_columns(dpairs_t_ref, place_ref[0] * half, half).T
+    target_grad_ref[...] = (
+        grad_first_ref[own_rows, :]
+        + dot_nt(dquery_ref[own_rows, :], self_in_ref[:, :width])
+        + dot_nt(own_dpairs, self_in_ref[:, width:])
+    )
+
+
+VMEM_LIMIT = 56 * 1024 * 1024
+
+
+def run_kernel(kernel, scalars, arrays, outs, scratch, flops):
+    in_specs = [pl.BlockSpec(memory_space=pltpu.SMEM)] * len(scalars)
+    in_specs += [pl.BlockSpec(memory_space=pltpu.VMEM)] * len(arrays)
+    shapes = [jax.ShapeDtypeStruct(shape, dtype) for shape, dtype in outs]
+    moved = sum(math.prod(s.shape) * s.dtype.itemsize for s in shapes)
+    moved += sum(math.prod(a.shape) * a.dtype.itemsize for a in arrays)
+    return pl.pallas_call(
+        kernel,
+        out_shape=shapes,
+        in_specs=in_specs,
+        out_specs=[pl.BlockSpec(memory_space=pltpu.VMEM)] * len(outs),
+        scratch_shapes=[pltpu.VMEM(shape, dtype) for shape, dtype in scratch],
+        compiler_params=pltpu.CompilerParams(vmem_limit_bytes=VMEM_LIMIT),
+        cost_estimate=pl.CostEstimate(flops=flops, bytes_accessed=moved, transcendentals=0),
+    )(*scalars, *arrays)
+
+
+def swap_wide(values, bit):
+    count = lax.axis_size("wide")
+    return lax.ppermute(values, "wide", [(i, i ^ bit) for i in range(count)])
+
+
+def wide_bits():
+    count = lax.axis_size("wide")
+    return [1 << k for k in range(count.bit_length() - 1)]
+
+
+def wide_total(keep, send):
+    here = lax.axis_index("wide")
+    bits = wide_bits()
+    total = keep.astype(jnp.float32) + swap_wide(send, bits[0]).astype(jnp.float32)
+    for bit in bits[1:]:
+        half = total.shape[0] // 2
+        side = (here // bit) % 2
+        other = lax.dynamic_slice_in_dim(total, (1 - side) * half, half, 0)
+        mine = lax.dynamic_slice_in_dim(total, side * half, half, 0)
+        total = mine + swap_wide(low(other), bit).astype(jnp.float32)
+    whole = low(total)
+    for bit in bits[::-1]:
+        side = (here // bit) % 2
+        theirs = swap_wide(whole, bit)
+        whole = jnp.where(
+            side == 0,
+            jnp.concatenate([whole, theirs], axis=0),
+            jnp.concatenate([theirs, whole], axis=0),
+        )
+    return whole
+
+
+def wide_total_small(values):
+    for bit in wide_bits():
+        values = values + swap_wide(values, bit)
+    return values
+
+
+def whole_rows(
+    target, memory, target_lens, source_lens, self_in, self_out, cross_q, cross_kv, cross_out, ffn_in, ffn_in_bias,
+    ffn_out, ffn_out_bias, norm_gain, norm_bias, cotangent,
+):
+    f32, bf16 = jnp.float32, jnp.bfloat16
+    _, half, width = target.shape
+    length = 2 * half
+    hidden = ffn_in.shape[1]
+    narrow = lax.axis_index("narrow")
+    place = jnp.stack([narrow, lax.axis_index("wide") % 2]).astype(jnp.int32)
+
+    def other_half(values):
+        return lax.ppermute(values, "narrow", [(0, 1), (1, 0)])
+
+    own_t, own_m, own_c = target[0], memory[0], cotangent[0]
+    other_t, other_m, other_c = other_half(own_t), other_half(own_m), other_half(own_c)
+    square = (length, width)
+    attn_shape = (HEADS, length, length)
+    macs = length * width * width
+    triple, self_attn, self_mix, unit_first, scale_first = run_kernel(
+        self_forward_kernel,
+        (place, target_lens),
+        (own_t, other_t, self_in, self_out),
+        [((length, 3 * width), bf16), (attn_shape, bf16), (square, bf16), (square, f32), ((length, 1), f32)],
+        [(square, bf16), ((length, length), f32)],
+        16 * macs,
+    )
+    query, pairs, cross_attn, cross_mix, unit_second, scale_second = run_kernel(
+        cross_forward_kernel,
+        (place, target_lens, source_lens),
+        (own_m, other_m, unit_first, cross_q, cross_kv, cross_out, norm_gain, norm_bias),
+        [
+            (square, bf16), ((length, 2 * width), bf16), (attn_shape, bf16), (square, bf16),
+            (square, f32), ((length, 1), f32),
+        ],
+        [(square, bf16), ((length, length), f32)],
+        16 * macs,
+    )
+    (
+        output, out_keep, out_send, in_keep, in_send, in_bias_g, norm_third_g, grad_second,
+    ) = run_kernel(
+        feed_kernel,
+        (place,),
+        (
+            own_c, other_c, unit_second, scale_second, ffn_in, ffn_in_bias[None], ffn_out, ffn_out_bias[None],
+            norm_gain, norm_bias,
+        ),
+        [
+            ((half, width), bf16),
+            ((hidden // 4, width), f32), ((hidden // 4, width), bf16),
+            ((width // 4, hidden), f32), ((width // 4, hidden), bf16),
+            ((1, hidden), f32), ((8, width), f32), (square, f32),
+        ],
+        [
+            (square, bf16), (square, bf16), ((length, hidden), bf16), ((length, hidden), f32),
+            (square, bf16), ((length, hidden), bf16),
+        ],
+        40 * macs,
+    )
+    ffn_out_g = wide_total(out_keep, out_send)
+    ffn_in_g = wide_total(in_keep, in_send)
+    cross_keep, cross_send, memory_grad, norm_first_g, grad_first = run_kernel(
+        cross_back_kernel,
+        (place, target_lens, source_lens),
+        (
+            own_m, other_m, grad_second, unit_first, scale_first, query, pairs, cross_attn, cross_mix,
+            cross_q, cross_kv, cross_out, norm_gain, norm_bias,
+        ),
+        [
+            ((width // 4, 4 * width), f32), ((width // 4, 4 * width), bf16), ((half, width), f32),
+            ((8, width), f32), (square, f32),
+        ],
+        [
+            (square, bf16), (square, bf16), (square, bf16), (square, bf16), (square, bf16), (square, bf16),
+            (square, bf16), ((2 * width, length), bf16),
+        ],
+        32 * macs,
+    )
+    cross_g = wide_total(cross_keep, cross_send)
+    self_keep, self_send, target_grad = run_kernel(
+        self_back_kernel,
+        (place,),
+        (own_t, other_t, grad_first, triple, self_attn, self_mix, self_in, self_out),
+        [
+            ((width // 4, 4 * width), f32), ((width // 4, 4 * width), bf16), ((half, width), f32),
+        ],
+        [
+            (square, bf16), (square, bf16), (square, bf16), (square, bf16), (square, bf16),
+            (square, bf16), ((2 * width, length), bf16),
+        ],
+        32 * macs,
+    )
+    self_g = wide_total(self_keep, self_send)
+    vectors = jnp.concatenate([in_bias_g.reshape(-1, width), norm_third_g, norm_first_g], axis=0)
+    vectors = wide_total_small(vectors)
+    count = hidden // width
+    in_bias_g, norm_g = vectors[:count].reshape(-1), vectors[count:]
+
+    def own_part(values):
+        size = values.shape[-1] // 2
+        return lax.dynamic_slice_in_dim(values, narrow * size, size, values.ndim - 1)
+
+    gain_g = own_part(jnp.stack([norm_g[8], norm_g[2], norm_g[0]]))
+    shift_g = own_part(jnp.stack([norm_g[9], norm_g[3], norm_g[1]]))
+    return (
+        output[None],
+        target_grad[None],
+        memory_grad[None],
+        self_g[:, : 3 * width].astype(f32),
+        self_g[:, 3 * width :].astype(f32),
+        cross_g[:, :width].astype(f32),
+        cross_g[:, width : 3 * width].astype(f32),
+        cross_g[:, 3 * width :].astype(f32),
+        ffn_in_g.astype(f32),
+        own_part(in_bias_g),
+        ffn_out_g.astype(f32),
+        own_part(norm_g[4]),
+        gain_g,
+        shift_g,
+    )
+
+
+def fits_whole_rows(mesh, target):
+    wide, narrow = mesh.shape["wide"], mesh.shape["narrow"]
+    rows, length, width = target.shape
+    return (
+        narrow == 2
+        and rows == wide
+        and wide >= 2
+        and wide & (wide - 1) == 0
+        and length <= 512
+        and width == HEADS * HEAD_DIM
+        and width % (16 * wide) == 0
+    )
+
+
 def solution(mesh):
     in_specs = (
         P("wide", "narrow", None),
@@ -404,4 +921,9 @@
         P(None, "narrow"),
         P(None, "narrow"),
     )
-    return jax.shard_map(local, mesh=mesh, in_specs=in_specs, out_specs=out_specs, check_vma=False)
+
+    def layer(*arrays):
+        body = whole_rows if fits_whole_rows(mesh, arrays[0]) else local
+        return jax.shard_map(body, mesh=mesh, in_specs=in_specs, out_specs=out_specs, check_vma=False)(*arrays)
+
+    return layer

time: 481 us -> 181 us (0.38)
  waiting for transfers between devices: 311 us -> 61 us
  matrix products: 60.3 us -> 0 us
  Pallas kernels: 0 us -> 59.5 us
  blocking collectives: 39.9 us -> 0 us
  starting transfers between devices: 0.8 us -> 40.6 us
  local copies, waits for them, and re-layouts: 28.6 us -> 4.14 us
  between operations: 16.3 us -> 1.13 us
  other arithmetic: 22.9 us -> 13.9 us
    reduce_scatter x9 -> x0, waiting for transfers between devices: 179 us -> none  [the longest x1 34.8 us: local(): lax.psum_scatter(ffn_out_g.astype(jnp.bfloat16), 'narrow', scatter_dimens...]
    psum x1 -> x0, waiting for transfers between devices: 77.3 us -> none  [local(): lax.psum(sh_a.astype(jnp.bfloat16), 'wide').astype(jnp.float32)]
    ppermute x0 -> x39, waiting for transfers between devices: none -> 61 us  [the longest x36 56.2 us: swap_wide(): return lax.ppermute(values, 'wide', [(i, i ^ bit) for i in range(count)])]
    dot_general x33 -> x0, matrix products: 60.3 us -> none  [the longest x7 19.7 us: weight_grad(): jnp.einsum('rsd,rse->de', activity, gradient, preferred_element_type=jnp....]
    pallas_call x0 -> x5, Pallas kernels: none -> 59.5 us  [run_kernel(): pl.pallas_call(kernel, out_shape=shapes, in_specs=in_specs, out_specs=[pl...]
    ppermute x0 -> x39, starting transfers between devices: none -> 40.6 us  [the longest x36 35.5 us: swap_wide(): return lax.ppermute(values, 'wide', [(i, i ^ bit) for i in range(count)])]
    all_gather x2 -> x0, waiting for transfers between devices: 36.7 us -> none  [the longest x1 18.4 us: local(): lax.all_gather(cross_pairs, 'narrow', axis=1, tiled=True)]
    psum x1 -> x0, blocking collectives: 34.9 us -> none  [local(): lax.psum(sh_g.astype(jnp.bfloat16), 'wide').astype(jnp.float32)]
  transfers between devices with their start and end apart: 14 -> 39, of which waited for: 13 -> 23; matrix products, arithmetic and copies ran while one was open for 11% -> 6% of each run, Pallas kernels for 0% -> 18%
where the time goes in v1:
time: 181 us; the launch traced here: 180 us
  waiting for transfers between devices  61 us (34%)
  Pallas kernels  59.5 us (33%)
  starting transfers between devices  40.6 us (22%)
  other arithmetic  13.9 us (8%)
  local copies, waits for them, and re-layouts  4.14 us (2%)
    pallas_call x5, Pallas kernels, run_kernel(): pl.pallas_call(kernel, out_shape=shapes, in_specs=in_specs, out_specs=[pl...  59.5 us
    ppermute x36, waiting for transfers between devices, swap_wide(): return lax.ppermute(values, 'wide', [(i, i ^ bit) for i in range(count)])  56.2 us
    ppermute x36, starting transfers between devices, swap_wide(): return lax.ppermute(values, 'wide', [(i, i ^ bit) for i in range(count)])  35.5 us
    ppermute x3, starting transfers between devices, other_half(): return lax.ppermute(values, 'narrow', [(0, 1), (1, 0)])  5.03 us
    ppermute x3, waiting for transfers between devices, other_half(): return lax.ppermute(values, 'narrow', [(0, 1), (1, 0)])  4.74 us
  transfers between devices with their start and end apart: 39, of which 23 were waited for; matrix products, arithmetic and copies ran while one was open for 6% of the time, Pallas kernels for 18%

profile of v1, /device:TPU:0, one launch (start us, length us, event | category | flops | bytes accessed | tf_op | source)
XLA Modules:
  0.0 180.2 jit_solution(10153034793950397472)
XLA Ops:
  0.6 3.0 %collective-permute-start.2 = (bf16[256,512]{1,0:T(8,128)(2,1)}, bf16[256,512]{1,0:T(8,128)(2,1)S(1)}, u32[]{:S(2)}, u32[]{:S(2)}) collective-permute-start(bf16[256,512]{1,0:T(8,128)(2,1)} %bitcast.21), channel_id=1, source_target_pairs={{0,1},{1,0},{2,3},{3,2},{4,5},{5,4},{6,7},{7,6},{8,9},{9,8},{10,11... | collective-permute-start | bytes 786440 | tf_op jit(solution)/shard_map/ppermute | solution.py:765
  3.7 1.9 %collective-permute-start = (bf16[256,512]{1,0:T(8,128)(2,1)}, bf16[256,512]{1,0:T(8,128)(2,1)S(1)}, u32[]{:S(2)}, u32[]{:S(2)}) collective-permute-start(bf16[256,512]{1,0:T(8,128)(2,1)} %bitcast.16), channel_id=1, source_target_pairs={{0,1},{1,0},{2,3},{3,2},{4,5},{5,4},{6,7},{7,6},{8,9},{9,8},{10,11... | collective-permute-start | bytes 786440 | tf_op jit(solution)/shard_map/ppermute | solution.py:765
  5.7 0.6 pad_add_fusion.place_ref
  6.3 4.7 %collective-permute-done.2.other_ref = bf16[256,512]{1,0:T(8,128)(2,1)S(1)} collective-permute-done((bf16[256,512]{1,0:T(8,128)(2,1)}, bf16[256,512]{1,0:T(8,128)(2,1)S(1)}, u32[]{:S(2)}, u32[]{:S(2)}) %collective-permute-start.2) | collective-permute-done | bytes 262176 | tf_op jit(solution)/shard_map/ppermute | solution.py:765
  11.0 0.7 copy-done.7
  11.7 10.2 %shard_map.263 = (bf16[512,1536]{1,0:T(8,128)(2,1)}, bf16[8,512,512]{2,1,0:T(8,128)(2,1)}, bf16[512,512]{1,0:T(8,128)(2,1)}, f32[512,512]{1,0:T(8,128)}, f32[512,1]{1,0:T(8,128)}) custom-call(s32[2]{0:T(128)} %pad_add_fusion.place_ref, s32[1,8]{1,0:T(1,128)} %target_lens_ref.3, bf16[256,512]{1,0:T(8,128)(2,1)} %bitcast.22, bf16[256,512]{1,0:T(8,128)(2,1)} %copy-done.7, ...), custom_call_target="tpu_custom_call" | custom-call | flops 2147483648 | bytes 9963520 | tf_op jit(solution)/shard_map/pallas_call | solution.py:704
  21.9 0.7 copy-done.8
  22.6 11.8 %shard_map.264 = (bf16[512,512]{1,0:T(8,128)(2,1)}, bf16[512,1024]{1,0:T(8,128)(2,1)}, bf16[8,512,512]{2,1,0:T(8,128)(2,1)}, bf16[512,512]{1,0:T(8,128)(2,1)}, f32[512,512]{1,0:T(8,128)}, /*index=5*/f32[512,1]{1,0:T(8,128)}) custom-call(s32[2]{0:T(128)} %pad_add_fusion.place_ref, s32[1,8]{1,0:T(1,128)} %target_lens_ref.3, s32[1,8]{1,0:T(1,128)} %source_lens_ref.3, ...), custom_call_target="tpu_custom_call" | custom-call | flops 2147483648 | bytes 11024384 | tf_op jit(solution)/shard_map/pallas_call | solution.py:704
  34.5 0.7 copy-done.9
  35.2 12.3 %shard_map.265 = (bf16[256,512]{1,0:T(8,128)(2,1)}, f32[512,512]{1,0:T(8,128)}, bf16[512,512]{1,0:T(8,128)(2,1)}, f32[128,2048]{1,0:T(8,128)}, bf16[128,2048]{1,...) custom-call(s32[2]{0:T(128)} %pad_add_fusion.place_ref, bf16[256,512]{1,0:T(8,128)(2,1)} %bitcast.17, ...), custom_call_target="tpu_custom_call" | custom-call | flops 5368709120 | bytes 10272768 | tf_op jit(solution)/shard_map/pallas_call | solution.py:704
  47.9 1.4 reduce.3
  49.4 14.0 %shard_map.266 = (f32[128,2048]{1,0:T(8,128)}, bf16[128,2048]{1,0:T(8,128)(2,1)}, f32[256,512]{1,0:T(8,128)}, f32[8,512]{1,0:T(8,128)}, f32[512,512]{1,0:T(8,128)}) custom-call(s32[2]{0:T(128)} %pad_add_fusion.place_ref, s32[1,8]{1,0:T(1,128)} %target_lens_ref.3, s32[1,8]{1,0:T(1,128)} %source_lens_ref.3, bf16[256,512]{1,0:T(8,128)(2,1)} %bitcast.20, ...), custom_call_target="tpu_custom_call" | custom-call | flops 4294967296 | bytes 14186496 | tf_op jit(solution)/shard_map/pallas_call | solution.py:704
  63.4 0.7 pad_maximum_fusion
  64.2 1.2 collective-permute-done.27
  65.4 0.7 fusion.6
  66.2 2.1 %collective-permute-start.28 = (f32[20,512]{1,0:T(8,128)S(1)}, f32[20,512]{1,0:T(8,128)S(1)}, u32[]{:S(2)}, u32[]{:S(2)}) collective-permute-start(f32[20,512]{1,0:T(8,128)S(1)} %fusion.6), channel_id=1, source_target_pairs={{0,4},{2,6},{4,0},{6,2},{8,12},{10,14},{12,8},{14,10},{16,20},{18,... | collective-permute-start | bytes 122888 | tf_op jit(solution)/shard_map/ppermute | solution.py:717
  68.3 2.1 %collective-permute-done.28 = f32[20,512]{1,0:T(8,128)S(1)} collective-permute-done((f32[20,512]{1,0:T(8,128)S(1)}, f32[20,512]{1,0:T(8,128)S(1)}, u32[]{:S(2)}, u32[]{:S(2)}) %collective-permute-start.28) | collective-permute-done | bytes 40992 | tf_op jit(solution)/shard_map/ppermute | solution.py:717
  70.4 2.1 %collective-permute-start.29 = (f32[20,512]{1,0:T(8,128)S(1)}, f32[20,512]{1,0:T(8,128)S(1)}, u32[]{:S(2)}, u32[]{:S(2)}) collective-permute-start(f32[20,512]{1,0:T(8,128)S(1)} %add.181), channel_id=1, source_target_pairs={{0,8},{2,10},{4,12},{6,14},{8,0},{10,2},{12,4},{14,6},{16,24},{18,... | collective-permute-start | bytes 122888 | tf_op jit(solution)/shard_map/ppermute | solution.py:717
  73.1 1.5 collective-permute-done.29
  74.6 3.1 %collective-permute-start.30 = (f32[20,512]{1,0:T(8,128)S(1)}, f32[20,512]{1,0:T(8,128)S(1)}, u32[]{:S(2)}, u32[]{:S(2)}) collective-permute-start(f32[20,512]{1,0:T(8,128)S(1)} %add.182), channel_id=1, source_target_pairs={{0,16},{2,18},{4,20},{6,22},{8,24},{10,26},{12,28},{14,30},{16,0},... | collective-permute-start | bytes 122888 | tf_op jit(solution)/shard_map/ppermute | solution.py:717
  77.7 11.1 %shard_map.267 = (f32[128,2048]{1,0:T(8,128)}, bf16[128,2048]{1,0:T(8,128)(2,1)}, f32[256,512]{1,0:T(8,128)}) custom-call(s32[2]{0:T(128)} %pad_add_fusion.place_ref, bf16[256,512]{1,0:T(8,128)(2,1)} %bitcast.23, bf16[256,512]{1,0:T(8,128)(2,1)} %copy-done.7, f32[512,512]{1,0:T(8,128)} %get-tuple-element.51.grad_first_ref, ...), custom_call_target="tpu_custom_call" | custom-call | flops 4294967296 | bytes 12058624 | tf_op jit(solution)/shard_map/pallas_call | solution.py:704
  88.9 0.6 constant_dynamic-slice_fusion
  89.5 0.6 dynamic_slice.104
  90.1 0.7 fusion.3
  91.0 1.6 collective-permute-start.32
  92.8 0.6 collective-permute-start.20
  93.5 1.5 collective-permute-start.12
  95.2 0.6 collective-permute-start.4
  95.9 4.3 %collective-permute-done.32 = bf16[256,512]{1,0:T(8,128)(2,1)S(1)} collective-permute-done((bf16[256,512]{1,0:T(8,128)(2,1)S(1)}, bf16[256,512]{1,0:T(8,128)(2,1)S(1)}, u32[]{:S(2)}, u32[]{:S(2)}) %collective-permute-start.32) | collective-permute-done | bytes 262176 | tf_op jit(solution)/shard_map/ppermute | solution.py:717
  100.3 1.6 collective-permute-start.33
  101.9 3.9 %collective-permute-done.20 = bf16[64,2048]{1,0:T(8,128)(2,1)S(1)} collective-permute-done((bf16[64,2048]{1,0:T(8,128)(2,1)S(1)}, bf16[64,2048]{1,0:T(8,128)(2,1)S(1)}, u32[]{:S(2)}, u32[]{:S(2)}) %collective-permute-start.20) | collective-permute-done | bytes 262176 | tf_op jit(solution)/shard_map/ppermute | solution.py:717
  105.9 1.6 collective-permute-start.21
  107.5 3.9 %collective-permute-done.12 = bf16[64,2048]{1,0:T(8,128)(2,1)S(1)} collective-permute-done((bf16[64,2048]{1,0:T(8,128)(2,1)S(1)}, bf16[64,2048]{1,0:T(8,128)(2,1)S(1)}, u32[]{:S(2)}, u32[]{:S(2)}) %collective-permute-start.12) | collective-permute-done | bytes 262176 | tf_op jit(solution)/shard_map/ppermute | solution.py:717
  111.5 1.6 collective-permute-start.13
  113.1 3.5 %collective-permute-done.4 = bf16[64,2048]{1,0:T(8,128)(2,1)S(1)} collective-permute-done((bf16[64,2048]{1,0:T(8,128)(2,1)S(1)}, bf16[64,2048]{1,0:T(8,128)(2,1)S(1)}, u32[]{:S(2)}, u32[]{:S(2)}) %collective-permute-start.4) | collective-permute-done | bytes 262176 | tf_op jit(solution)/shard_map/ppermute | solution.py:717
  116.7 1.6 collective-permute-start.5
  118.9 2.6 %collective-permute-start.22 = (bf16[16,2048]{1,0:T(8,128)(2,1)S(1)}, bf16[16,2048]{1,0:T(8,128)(2,1)S(1)}, u32[]{:S(2)}, u32[]{:S(2)}) collective-permute-start(bf16[16,2048]{1,0:T(8,128)(2,1)S(1)} %dynamic-slice_convert_fusion.9), channel_id=1, source_target_pairs={{0,16},{2,18},{4,20},{6,22},{8,24},{10,26},{12,28},{14,30},{16,0},... | collective-permute-start | bytes 196616 | tf_op jit(solution)/shard_map/ppermute | solution.py:717
  122.3 2.4 %collective-permute-start.6 = (bf16[16,2048]{1,0:T(8,128)(2,1)S(1)}, bf16[16,2048]{1,0:T(8,128)(2,1)S(1)}, u32[]{:S(2)}, u32[]{:S(2)}) collective-permute-start(bf16[16,2048]{1,0:T(8,128)(2,1)S(1)} %dynamic-slice_convert_fusion.11), channel_id=1, source_target_pairs={{0,16},{2,18},{4,20},{6,22},{8,24},{10,26},{12,28},{14,30},{16,0},... | collective-permute-start | bytes 196616 | tf_op jit(solution)/shard_map/ppermute | solution.py:717
  124.7 6.0 %collective-permute-done.34 = bf16[64,512]{1,0:T(8,128)(2,1)S(1)} collective-permute-done((bf16[64,512]{1,0:T(8,128)(2,1)S(1)}, bf16[64,512]{1,0:T(8,128)(2,1)S(1)}, u32[]{:S(2)}, u32[]{:S(2)}) %collective-permute-start.34) | collective-permute-done | bytes 65568 | tf_op jit(solution)/shard_map/ppermute | solution.py:717
  130.8 1.3 collective-permute-done.22
  132.1 1.7 collective-permute-start.23
  133.8 1.1 collective-permute-done.14
  135.2 2.5 %collective-permute-done.6 = bf16[16,2048]{1,0:T(8,128)(2,1)S(1)} collective-permute-done((bf16[16,2048]{1,0:T(8,128)(2,1)S(1)}, bf16[16,2048]{1,0:T(8,128)(2,1)S(1)}, u32[]{:S(2)}, u32[]{:S(2)}) %collective-permute-start.6) | collective-permute-done | bytes 65568 | tf_op jit(solution)/shard_map/ppermute | solution.py:717
  138.0 1.8 %collective-permute-done.35 = bf16[64,512]{1,0:T(8,128)(2,1)S(1)} collective-permute-done((bf16[64,512]{1,0:T(8,128)(2,1)S(1)}, bf16[64,512]{1,0:T(8,128)(2,1)S(1)}, u32[]{:S(2)}, u32[]{:S(2)}) %collective-permute-start.35) | collective-permute-done | bytes 65568 | tf_op jit(solution)/shard_map/ppermute | solution.py:717
  140.0 1.3 collective-permute-done.23
  141.3 0.8 collective-permute-start.24
  142.1 0.6 collective-permute-done.15
  142.7 0.7 collective-permute-start.16
  144.0 0.9 collective-permute-start.8
  144.9 1.8 %collective-permute-done.36 = bf16[128,512]{1,0:T(8,128)(2,1)S(1)} collective-permute-done((bf16[128,512]{1,0:T(8,128)(2,1)S(1)}, bf16[128,512]{1,0:T(8,128)(2,1)S(1)}, u32[]{:S(2)}, u32[]{:S(2)}) %collective-permute-start.36) | collective-permute-done | bytes 131104 | tf_op jit(solution)/shard_map/ppermute | solution.py:717
  146.8 1.6 collective-permute-start.37
  148.4 4.0 %collective-permute-done.16 = bf16[32,2048]{1,0:T(8,128)(2,1)S(1)} collective-permute-done((bf16[32,2048]{1,0:T(8,128)(2,1)S(1)}, bf16[32,2048]{1,0:T(8,128)(2,1)S(1)}, u32[]{:S(2)}, u32[]{:S(2)}) %collective-permute-start.16) | collective-permute-done | bytes 131104 | tf_op jit(solution)/shard_map/ppermute | solution.py:717
  152.4 1.6 collective-permute-start.17
  154.0 1.1 collective-permute-done.8
  155.1 1.6 collective-permute-start.9
  157.4 4.3 %collective-permute-done.17 = bf16[64,2048]{1,0:T(8,128)(2,1)S(1)} collective-permute-done((bf16[64,2048]{1,0:T(8,128)(2,1)S(1)}, bf16[64,2048]{1,0:T(8,128)(2,1)S(1)}, u32[]{:S(2)}, u32[]{:S(2)}) %collective-permute-start.17) | collective-permute-done | bytes 262176 | tf_op jit(solution)/shard_map/ppermute | solution.py:717
  161.9 5.4 %collective-permute-done.9 = bf16[64,2048]{1,0:T(8,128)(2,1)S(1)} collective-permute-done((bf16[64,2048]{1,0:T(8,128)(2,1)S(1)}, bf16[64,2048]{1,0:T(8,128)(2,1)S(1)}, u32[]{:S(2)}, u32[]{:S(2)}) %collective-permute-start.9) | collective-permute-done | bytes 262176 | tf_op jit(solution)/shard_map/ppermute | solution.py:717
  168.3 3.6 %collective-permute-done.25 = bf16[64,2048]{1,0:T(8,128)(2,1)S(1)} collective-permute-done((bf16[64,2048]{1,0:T(8,128)(2,1)S(1)}, bf16[64,2048]{1,0:T(8,128)(2,1)S(1)}, u32[]{:S(2)}, u32[]{:S(2)}) %collective-permute-start.25) | collective-permute-done | bytes 262176 | tf_op jit(solution)/shard_map/ppermute | solution.py:717
  172.6 0.9 slice_convert_fusion.4
  173.5 1.1 slice_convert_fusion.2
  174.6 1.1 slice_convert_fusion.1
  175.7 1.7 fusion.1
  177.3 1.3 slice_convert_fusion
  178.6 1.6 fusion
  (102 shorter events, 7.5 us)
Async XLA Ops:
  0.6 10.4 %collective-permute-start.2 = (bf16[256,512]{1,0:T(8,128)(2,1)}, bf16[256,512]{1,0:T(8,128)(2,1)S(1)}, u32[]{:S(2)}, u32[]{:S(2)}) collective-permute-start(bf16[256,512]{1,0:T(8,128)(2,1)} %bitcast.21), channel_id=1, source_target_pairs={{0,1},{1,0},{2,3},{3,2},{4,5},{5,4},{6,7},{7,6},{8,9},{9,8},{10,11... | collective-permute-start | bytes 786440 | tf_op jit(solution)/shard_map/ppermute | solution.py:765
  3.6 18.3 %collective-permute-start.1 = (bf16[256,512]{1,0:T(8,128)(2,1)}, bf16[256,512]{1,0:T(8,128)(2,1)S(1)}, u32[]{:S(2)}, u32[]{:S(2)}) collective-permute-start(bf16[256,512]{1,0:T(8,128)(2,1)} %bitcast.18), channel_id=1, source_target_pairs={{0,1},{1,0},{2,3},{3,2},{4,5},{5,4},{6,7},{7,6},{8,9},{9,8},{10,11... | collective-permute-start | bytes 786440 | tf_op jit(solution)/shard_map/ppermute | solution.py:765
  3.7 30.7 %collective-permute-start = (bf16[256,512]{1,0:T(8,128)(2,1)}, bf16[256,512]{1,0:T(8,128)(2,1)S(1)}, u32[]{:S(2)}, u32[]{:S(2)}) collective-permute-start(bf16[256,512]{1,0:T(8,128)(2,1)} %bitcast.16), channel_id=1, source_target_pairs={{0,1},{1,0},{2,3},{3,2},{4,5},{5,4},{6,7},{7,6},{8,9},{9,8},{10,11... | collective-permute-start | bytes 786440 | tf_op jit(solution)/shard_map/ppermute | solution.py:765
  11.0 0.7 copy-start.7
  21.9 0.7 copy-start.8
  34.4 0.7 copy-start.9
  49.3 14.1 %copy-start.4 = (f32[8,512]{1,0:T(8,128)S(1)}, f32[8,512]{1,0:T(8,128)}, u32[]{:S(2)}) copy-start(f32[8,512]{1,0:T(8,128)} %get-tuple-element.64) | copy-start | bytes 49156
  49.3 23.2 %copy-start.6 = (bf16[512,512]{1,0:T(8,128)(2,1)S(1)}, bf16[512,512]{1,0:T(8,128)(2,1)}, u32[]{:S(2)}) copy-start(bf16[512,512]{1,0:T(8,128)(2,1)} %get-tuple-element.67) | copy-start | bytes 1572868
  49.3 23.2 %copy-start.5 = (bf16[128,2048]{1,0:T(8,128)(2,1)S(1)}, bf16[128,2048]{1,0:T(8,128)(2,1)}, u32[]{:S(2)}) copy-start(bf16[128,2048]{1,0:T(8,128)(2,1)} %get-tuple-element.62) | copy-start | bytes 1572868
  64.1 1.3 collective-permute-start.27
  66.2 4.2 %collective-permute-start.28 = (f32[20,512]{1,0:T(8,128)S(1)}, f32[20,512]{1,0:T(8,128)S(1)}, u32[]{:S(2)}, u32[]{:S(2)}) collective-permute-start(f32[20,512]{1,0:T(8,128)S(1)} %fusion.6), channel_id=1, source_target_pairs={{0,4},{2,6},{4,0},{6,2},{8,12},{10,14},{12,8},{14,10},{16,20},{18,... | collective-permute-start | bytes 122888 | tf_op jit(solution)/shard_map/ppermute | solution.py:717
  70.4 4.2 %collective-permute-start.29 = (f32[20,512]{1,0:T(8,128)S(1)}, f32[20,512]{1,0:T(8,128)S(1)}, u32[]{:S(2)}, u32[]{:S(2)}) collective-permute-start(f32[20,512]{1,0:T(8,128)S(1)} %add.181), channel_id=1, source_target_pairs={{0,8},{2,10},{4,12},{6,14},{8,0},{10,2},{12,4},{14,6},{16,24},{18,... | collective-permute-start | bytes 122888 | tf_op jit(solution)/shard_map/ppermute | solution.py:717
  72.5 18.3 %collective-permute-start.31 = (bf16[512,512]{1,0:T(8,128)(2,1)S(1)}, bf16[512,512]{1,0:T(8,128)(2,1)S(1)}, u32[]{:S(2)}, u32[]{:S(2)}) collective-permute-start(bf16[512,512]{1,0:T(8,128)(2,1)S(1)} %copy-done.6), channel_id=1, source_target_pairs={{0,2},{2,0},{4,6},{6,4},{8,10},{10,8},{12,14},{14,12},{16,18},{18,... | collective-permute-start | bytes 1572872 | tf_op jit(solution)/shard_map/ppermute | solution.py:717
  72.5 20.0 %collective-permute-start.19 = (bf16[128,2048]{1,0:T(8,128)(2,1)S(1)}, bf16[128,2048]{1,0:T(8,128)(2,1)S(1)}, u32[]{:S(2)}, u32[]{:S(2)}) collective-permute-start(bf16[128,2048]{1,0:T(8,128)(2,1)S(1)} %copy-done.5), channel_id=1, source_target_pairs={{0,2},{2,0},{4,6},{6,4},{8,10},{10,8},{12,14},{14,12},{16,18},{18,... | collective-permute-start | bytes 1572872 | tf_op jit(solution)/shard_map/ppermute | solution.py:717
  73.0 20.3 %collective-permute-start.11 = (bf16[128,2048]{1,0:T(8,128)(2,1)}, bf16[128,2048]{1,0:T(8,128)(2,1)S(1)}, u32[]{:S(2)}, u32[]{:S(2)}) collective-permute-start(bf16[128,2048]{1,0:T(8,128)(2,1)} %get-tuple-element.60), channel_id=1, source_target_pairs={{0,2},{2,0},{4,6},{6,4},{8,10},{10,8},{12,14},{14,12},{16,18},{18,... | collective-permute-start | bytes 1572872 | tf_op jit(solution)/shard_map/ppermute | solution.py:717
  74.6 14.3 %collective-permute-start.30 = (f32[20,512]{1,0:T(8,128)S(1)}, f32[20,512]{1,0:T(8,128)S(1)}, u32[]{:S(2)}, u32[]{:S(2)}) collective-permute-start(f32[20,512]{1,0:T(8,128)S(1)} %add.182), channel_id=1, source_target_pairs={{0,16},{2,18},{4,20},{6,22},{8,24},{10,26},{12,28},{14,30},{16,0},... | collective-permute-start | bytes 122888 | tf_op jit(solution)/shard_map/ppermute | solution.py:717
  77.7 13.1 %copy-start.2 = (f32[512,512]{1,0:T(8,128)S(1)}, f32[512,512]{1,0:T(8,128)}, u32[]{:S(2)}) copy-start(f32[512,512]{1,0:T(8,128)} %get-tuple-element.66) | copy-start | bytes 3145732
  88.9 3.7 %copy-start = (f32[128,2048]{1,0:T(8,128)S(1)}, f32[128,2048]{1,0:T(8,128)}, u32[]{:S(2)}) copy-start(f32[128,2048]{1,0:T(8,128)} %get-tuple-element.61) | copy-start | bytes 3145732
  88.9 6.2 %collective-permute-start.3 = (bf16[128,2048]{1,0:T(8,128)(2,1)}, bf16[128,2048]{1,0:T(8,128)(2,1)S(1)}, u32[]{:S(2)}, u32[]{:S(2)}) collective-permute-start(bf16[128,2048]{1,0:T(8,128)(2,1)} %get-tuple-element.58), channel_id=1, source_target_pairs={{0,2},{2,0},{4,6},{6,4},{8,10},{10,8},{12,14},{14,12},{16,18},{18,... | collective-permute-start | bytes 1572872 | tf_op jit(solution)/shard_map/ppermute | solution.py:717
  91.0 2.4 %copy-start.1 = (f32[128,2048]{1,0:T(8,128)S(1)}, f32[128,2048]{1,0:T(8,128)}, u32[]{:S(2)}) copy-start(f32[128,2048]{1,0:T(8,128)} %get-tuple-element.59) | copy-start | bytes 3145732
  91.0 9.2 %collective-permute-start.32 = (bf16[256,512]{1,0:T(8,128)(2,1)S(1)}, bf16[256,512]{1,0:T(8,128)(2,1)S(1)}, u32[]{:S(2)}, u32[]{:S(2)}) collective-permute-start(bf16[256,512]{1,0:T(8,128)(2,1)S(1)} %dynamic-slice_convert_fusion), channel_id=1, source_target_pairs={{0,4},{2,6},{4,0},{6,2},{8,12},{10,14},{12,8},{14,10},{16,20},{18,... | collective-permute-start | bytes 786440 | tf_op jit(solution)/shard_map/ppermute | solution.py:717
  92.7 2.4 %copy-start.3 = (f32[128,2048]{1,0:T(8,128)S(1)}, f32[128,2048]{1,0:T(8,128)}, u32[]{:S(2)}) copy-start(f32[128,2048]{1,0:T(8,128)} %get-tuple-element.57) | copy-start | bytes 3145732
  92.8 13.1 %collective-permute-start.20 = (bf16[64,2048]{1,0:T(8,128)(2,1)S(1)}, bf16[64,2048]{1,0:T(8,128)(2,1)S(1)}, u32[]{:S(2)}, u32[]{:S(2)}) collective-permute-start(bf16[64,2048]{1,0:T(8,128)(2,1)S(1)} %dynamic-slice_convert_fusion.1), channel_id=1, source_target_pairs={{0,4},{2,6},{4,0},{6,2},{8,12},{10,14},{12,8},{14,10},{16,20},{18,... | collective-permute-start | bytes 786440 | tf_op jit(solution)/shard_map/ppermute | solution.py:717
  93.5 17.9 %collective-permute-start.12 = (bf16[64,2048]{1,0:T(8,128)(2,1)S(1)}, bf16[64,2048]{1,0:T(8,128)(2,1)S(1)}, u32[]{:S(2)}, u32[]{:S(2)}) collective-permute-start(bf16[64,2048]{1,0:T(8,128)(2,1)S(1)} %dynamic-slice_convert_fusion.2), channel_id=1, source_target_pairs={{0,4},{2,6},{4,0},{6,2},{8,12},{10,14},{12,8},{14,10},{16,20},{18,... | collective-permute-start | bytes 786440 | tf_op jit(solution)/shard_map/ppermute | solution.py:717
  95.2 21.4 %collective-permute-start.4 = (bf16[64,2048]{1,0:T(8,128)(2,1)S(1)}, bf16[64,2048]{1,0:T(8,128)(2,1)S(1)}, u32[]{:S(2)}, u32[]{:S(2)}) collective-permute-start(bf16[64,2048]{1,0:T(8,128)(2,1)S(1)} %dynamic-slice_convert_fusion.3), channel_id=1, source_target_pairs={{0,4},{2,6},{4,0},{6,2},{8,12},{10,14},{12,8},{14,10},{16,20},{18,... | collective-permute-start | bytes 786440 | tf_op jit(solution)/shard_map/ppermute | solution.py:717
  100.3 18.0 %collective-permute-start.33 = (bf16[128,512]{1,0:T(8,128)(2,1)S(1)}, bf16[128,512]{1,0:T(8,128)(2,1)S(1)}, u32[]{:S(2)}, u32[]{:S(2)}) collective-permute-start(bf16[128,512]{1,0:T(8,128)(2,1)S(1)} %dynamic-slice_convert_fusion.4), channel_id=1, source_target_pairs={{0,8},{2,10},{4,12},{6,14},{8,0},{10,2},{12,4},{14,6},{16,24},{18,... | collective-permute-start | bytes 393224 | tf_op jit(solution)/shard_map/ppermute | solution.py:717
  105.9 12.9 %collective-permute-start.21 = (bf16[32,2048]{1,0:T(8,128)(2,1)S(1)}, bf16[32,2048]{1,0:T(8,128)(2,1)S(1)}, u32[]{:S(2)}, u32[]{:S(2)}) collective-permute-start(bf16[32,2048]{1,0:T(8,128)(2,1)S(1)} %dynamic-slice_convert_fusion.5), channel_id=1, source_target_pairs={{0,8},{2,10},{4,12},{6,14},{8,0},{10,2},{12,4},{14,6},{16,24},{18,... | collective-permute-start | bytes 393224 | tf_op jit(solution)/shard_map/ppermute | solution.py:717
  111.5 10.0 %collective-permute-start.13 = (bf16[32,2048]{1,0:T(8,128)(2,1)S(1)}, bf16[32,2048]{1,0:T(8,128)(2,1)S(1)}, u32[]{:S(2)}, u32[]{:S(2)}) collective-permute-start(bf16[32,2048]{1,0:T(8,128)(2,1)S(1)} %dynamic-slice_convert_fusion.6), channel_id=1, source_target_pairs={{0,8},{2,10},{4,12},{6,14},{8,0},{10,2},{12,4},{14,6},{16,24},{18,... | collective-permute-start | bytes 393224 | tf_op jit(solution)/shard_map/ppermute | solution.py:717
  116.7 5.5 %collective-permute-start.5 = (bf16[32,2048]{1,0:T(8,128)(2,1)S(1)}, bf16[32,2048]{1,0:T(8,128)(2,1)S(1)}, u32[]{:S(2)}, u32[]{:S(2)}) collective-permute-start(bf16[32,2048]{1,0:T(8,128)(2,1)S(1)} %dynamic-slice_convert_fusion.7), channel_id=1, source_target_pairs={{0,8},{2,10},{4,12},{6,14},{8,0},{10,2},{12,4},{14,6},{16,24},{18,... | collective-permute-start | bytes 393224 | tf_op jit(solution)/shard_map/ppermute | solution.py:717
  118.4 12.3 %collective-permute-start.34 = (bf16[64,512]{1,0:T(8,128)(2,1)S(1)}, bf16[64,512]{1,0:T(8,128)(2,1)S(1)}, u32[]{:S(2)}, u32[]{:S(2)}) collective-permute-start(bf16[64,512]{1,0:T(8,128)(2,1)S(1)} %dynamic-slice_convert_fusion.8), channel_id=1, source_target_pairs={{0,16},{2,18},{4,20},{6,22},{8,24},{10,26},{12,28},{14,30},{16,0},... | collective-permute-start | bytes 196616 | tf_op jit(solution)/shard_map/ppermute | solution.py:717
  118.9 13.2 %collective-permute-start.22 = (bf16[16,2048]{1,0:T(8,128)(2,1)S(1)}, bf16[16,2048]{1,0:T(8,128)(2,1)S(1)}, u32[]{:S(2)}, u32[]{:S(2)}) collective-permute-start(bf16[16,2048]{1,0:T(8,128)(2,1)S(1)} %dynamic-slice_convert_fusion.9), channel_id=1, source_target_pairs={{0,16},{2,18},{4,20},{6,22},{8,24},{10,26},{12,28},{14,30},{16,0},... | collective-permute-start | bytes 196616 | tf_op jit(solution)/shard_map/ppermute | solution.py:717
  121.6 13.3 %collective-permute-start.14 = (bf16[16,2048]{1,0:T(8,128)(2,1)S(1)}, bf16[16,2048]{1,0:T(8,128)(2,1)S(1)}, u32[]{:S(2)}, u32[]{:S(2)}) collective-permute-start(bf16[16,2048]{1,0:T(8,128)(2,1)S(1)} %dynamic-slice_convert_fusion.10), channel_id=1, source_target_pairs={{0,16},{2,18},{4,20},{6,22},{8,24},{10,26},{12,28},{14,30},{16,0},... | collective-permute-start | bytes 196616 | tf_op jit(solution)/shard_map/ppermute | solution.py:717
  122.3 15.4 %collective-permute-start.6 = (bf16[16,2048]{1,0:T(8,128)(2,1)S(1)}, bf16[16,2048]{1,0:T(8,128)(2,1)S(1)}, u32[]{:S(2)}, u32[]{:S(2)}) collective-permute-start(bf16[16,2048]{1,0:T(8,128)(2,1)S(1)} %dynamic-slice_convert_fusion.11), channel_id=1, source_target_pairs={{0,16},{2,18},{4,20},{6,22},{8,24},{10,26},{12,28},{14,30},{16,0},... | collective-permute-start | bytes 196616 | tf_op jit(solution)/shard_map/ppermute | solution.py:717
  130.7 9.1 %collective-permute-start.35 = (bf16[64,512]{1,0:T(8,128)(2,1)S(1)}, bf16[64,512]{1,0:T(8,128)(2,1)S(1)}, u32[]{:S(2)}, u32[]{:S(2)}) collective-permute-start(bf16[64,512]{1,0:T(8,128)(2,1)S(1)} %add_convert_fusion), channel_id=1, source_target_pairs={{0,16},{2,18},{4,20},{6,22},{8,24},{10,26},{12,28},{14,30},{16,0},... | collective-permute-start | bytes 196616 | tf_op jit(solution)/shard_map/ppermute | solution.py:717
  132.1 9.1 %collective-permute-start.23 = (bf16[16,2048]{1,0:T(8,128)(2,1)S(1)}, bf16[16,2048]{1,0:T(8,128)(2,1)S(1)}, u32[]{:S(2)}, u32[]{:S(2)}) collective-permute-start(bf16[16,2048]{1,0:T(8,128)(2,1)S(1)} %add_convert_fusion.1), channel_id=1, source_target_pairs={{0,16},{2,18},{4,20},{6,22},{8,24},{10,26},{12,28},{14,30},{16,0},... | collective-permute-start | bytes 196616 | tf_op jit(solution)/shard_map/ppermute | solution.py:717
  135.0 7.7 %collective-permute-start.15 = (bf16[16,2048]{1,0:T(8,128)(2,1)S(1)}, bf16[16,2048]{1,0:T(8,128)(2,1)S(1)}, u32[]{:S(2)}, u32[]{:S(2)}) collective-permute-start(bf16[16,2048]{1,0:T(8,128)(2,1)S(1)} %add_convert_fusion.2), channel_id=1, source_target_pairs={{0,16},{2,18},{4,20},{6,22},{8,24},{10,26},{12,28},{14,30},{16,0},... | collective-permute-start | bytes 196616 | tf_op jit(solution)/shard_map/ppermute | solution.py:717
  137.8 6.2 %collective-permute-start.7 = (bf16[16,2048]{1,0:T(8,128)(2,1)S(1)}, bf16[16,2048]{1,0:T(8,128)(2,1)S(1)}, u32[]{:S(2)}, u32[]{:S(2)}) collective-permute-start(bf16[16,2048]{1,0:T(8,128)(2,1)S(1)} %add_convert_fusion.3), channel_id=1, source_target_pairs={{0,16},{2,18},{4,20},{6,22},{8,24},{10,26},{12,28},{14,30},{16,0},... | collective-permute-start | bytes 196616 | tf_op jit(solution)/shard_map/ppermute | solution.py:717
  139.9 6.9 %collective-permute-start.36 = (bf16[128,512]{1,0:T(8,128)(2,1)S(1)}, bf16[128,512]{1,0:T(8,128)(2,1)S(1)}, u32[]{:S(2)}, u32[]{:S(2)}) collective-permute-start(bf16[128,512]{1,0:T(8,128)(2,1)S(1)} %maximum_select_fusion.15), channel_id=1, source_target_pairs={{0,8},{2,10},{4,12},{6,14},{8,0},{10,2},{12,4},{14,6},{16,24},{18,... | collective-permute-start | bytes 393224 | tf_op jit(solution)/shard_map/ppermute | solution.py:717
  141.3 15.5 %collective-permute-start.24 = (bf16[32,2048]{1,0:T(8,128)(2,1)S(1)}, bf16[32,2048]{1,0:T(8,128)(2,1)S(1)}, u32[]{:S(2)}, u32[]{:S(2)}) collective-permute-start(bf16[32,2048]{1,0:T(8,128)(2,1)S(1)} %maximum_select_fusion.14), channel_id=1, source_target_pairs={{0,8},{2,10},{4,12},{6,14},{8,0},{10,2},{12,4},{14,6},{16,24},{18,... | collective-permute-start | bytes 393224 | tf_op jit(solution)/shard_map/ppermute | solution.py:717
  142.7 9.6 %collective-permute-start.16 = (bf16[32,2048]{1,0:T(8,128)(2,1)S(1)}, bf16[32,2048]{1,0:T(8,128)(2,1)S(1)}, u32[]{:S(2)}, u32[]{:S(2)}) collective-permute-start(bf16[32,2048]{1,0:T(8,128)(2,1)S(1)} %maximum_select_fusion.13), channel_id=1, source_target_pairs={{0,8},{2,10},{4,12},{6,14},{8,0},{10,2},{12,4},{14,6},{16,24},{18,... | collective-permute-start | bytes 393224 | tf_op jit(solution)/shard_map/ppermute | solution.py:717
  144.0 11.1 %collective-permute-start.8 = (bf16[32,2048]{1,0:T(8,128)(2,1)S(1)}, bf16[32,2048]{1,0:T(8,128)(2,1)S(1)}, u32[]{:S(2)}, u32[]{:S(2)}) collective-permute-start(bf16[32,2048]{1,0:T(8,128)(2,1)S(1)} %maximum_select_fusion.12), channel_id=1, source_target_pairs={{0,8},{2,10},{4,12},{6,14},{8,0},{10,2},{12,4},{14,6},{16,24},{18,... | collective-permute-start | bytes 393224 | tf_op jit(solution)/shard_map/ppermute | solution.py:717
  146.8 20.7 %collective-permute-start.37 = (bf16[256,512]{1,0:T(8,128)(2,1)S(1)}, bf16[256,512]{1,0:T(8,128)(2,1)S(1)}, u32[]{:S(2)}, u32[]{:S(2)}) collective-permute-start(bf16[256,512]{1,0:T(8,128)(2,1)S(1)} %maximum_select_fusion.11), channel_id=1, source_target_pairs={{0,4},{2,6},{4,0},{6,2},{8,12},{10,14},{12,8},{14,10},{16,20},{18,... | collective-permute-start | bytes 786440 | tf_op jit(solution)/shard_map/ppermute | solution.py:717
  152.4 9.2 %collective-permute-start.17 = (bf16[64,2048]{1,0:T(8,128)(2,1)S(1)}, bf16[64,2048]{1,0:T(8,128)(2,1)S(1)}, u32[]{:S(2)}, u32[]{:S(2)}) collective-permute-start(bf16[64,2048]{1,0:T(8,128)(2,1)S(1)} %maximum_select_fusion.9), channel_id=1, source_target_pairs={{0,4},{2,6},{4,0},{6,2},{8,12},{10,14},{12,8},{14,10},{16,20},{18,... | collective-permute-start | bytes 786440 | tf_op jit(solution)/shard_map/ppermute | solution.py:717
  155.1 12.2 %collective-permute-start.9 = (bf16[64,2048]{1,0:T(8,128)(2,1)S(1)}, bf16[64,2048]{1,0:T(8,128)(2,1)S(1)}, u32[]{:S(2)}, u32[]{:S(2)}) collective-permute-start(bf16[64,2048]{1,0:T(8,128)(2,1)S(1)} %maximum_select_fusion.8), channel_id=1, source_target_pairs={{0,4},{2,6},{4,0},{6,2},{8,12},{10,14},{12,8},{14,10},{16,20},{18,... | collective-permute-start | bytes 786440 | tf_op jit(solution)/shard_map/ppermute | solution.py:717
  156.8 15.1 %collective-permute-start.25 = (bf16[64,2048]{1,0:T(8,128)(2,1)S(1)}, bf16[64,2048]{1,0:T(8,128)(2,1)S(1)}, u32[]{:S(2)}, u32[]{:S(2)}) collective-permute-start(bf16[64,2048]{1,0:T(8,128)(2,1)S(1)} %maximum_select_fusion.10), channel_id=1, source_target_pairs={{0,4},{2,6},{4,0},{6,2},{8,12},{10,14},{12,8},{14,10},{16,20},{18,... | collective-permute-start | bytes 786440 | tf_op jit(solution)/shard_map/ppermute | solution.py:717
  161.8 10.3 %collective-permute-start.18 = (bf16[128,2048]{1,0:T(8,128)(2,1)S(1)}, bf16[128,2048]{1,0:T(8,128)(2,1)S(1)}, u32[]{:S(2)}, u32[]{:S(2)}) collective-permute-start(bf16[128,2048]{1,0:T(8,128)(2,1)S(1)} %maximum_select_fusion.5), channel_id=1, source_target_pairs={{0,2},{2,0},{4,6},{6,4},{8,10},{10,8},{12,14},{14,12},{16,18},{18,... | collective-permute-start | bytes 1572872 | tf_op jit(solution)/shard_map/ppermute | solution.py:717
  167.4 4.9 %collective-permute-start.10 = (bf16[128,2048]{1,0:T(8,128)(2,1)S(1)}, bf16[128,2048]{1,0:T(8,128)(2,1)S(1)}, u32[]{:S(2)}, u32[]{:S(2)}) collective-permute-start(bf16[128,2048]{1,0:T(8,128)(2,1)S(1)} %maximum_select_fusion.4), channel_id=1, source_target_pairs={{0,2},{2,0},{4,6},{6,4},{8,10},{10,8},{12,14},{14,12},{16,18},{18,... | collective-permute-start | bytes 1572872 | tf_op jit(solution)/shard_map/ppermute | solution.py:717
  167.7 7.9 %collective-permute-start.38 = (bf16[512,512]{1,0:T(8,128)(2,1)S(1)}, bf16[512,512]{1,0:T(8,128)(2,1)S(1)}, u32[]{:S(2)}, u32[]{:S(2)}) collective-permute-start(bf16[512,512]{1,0:T(8,128)(2,1)S(1)} %maximum_select_fusion.7), channel_id=1, source_target_pairs={{0,2},{2,0},{4,6},{6,4},{8,10},{10,8},{12,14},{14,12},{16,18},{18,... | collective-permute-start | bytes 1572872 | tf_op jit(solution)/shard_map/ppermute | solution.py:717
  172.0 6.7 %collective-permute-start.26 = (bf16[128,2048]{1,0:T(8,128)(2,1)S(1)}, bf16[128,2048]{1,0:T(8,128)(2,1)S(1)}, u32[]{:S(2)}, u32[]{:S(2)}) collective-permute-start(bf16[128,2048]{1,0:T(8,128)(2,1)S(1)} %maximum_select_fusion.6), channel_id=1, source_target_pairs={{0,2},{2,0},{4,6},{6,4},{8,10},{10,8},{12,14},{14,12},{16,18},{18,... | collective-permute-start | bytes 1572872 | tf_op jit(solution)/shard_map/ppermute | solution.py:717
